TPU v7x, 32 devices: a whole 2x2x4 slice. The times are simulated.
32 devices in a mesh: section: 2 (over core), ctx: 4 (over z), fsdp: 4 (over y, x).
Axes of the slice: x: 2, y: 2, z: 4, core: 2. Of those that a mesh axis runs over, the one named last changes fastest.
Arguments:
- block_input: bfloat16 [1, 4, 512, 576], P(None, 'fsdp', 'ctx'), may hold values from -6 to 6
- cotangent: bfloat16 [1, 4, 512, 576], P(None, 'fsdp', 'ctx'), may hold values from -6 to 6
- span_order: int32 [8], replicated, may hold values from 0 to 7, as said below
- rope_ids: int32 [1, 4, 512], P(None, 'fsdp', 'ctx'), may hold values from 0 to 511, as said below
- norm_in: float32 [2, 576], P('section'), may hold values from 0.5 to 1.5
- w_query: bfloat16 [2, 576, 576], P('section', 'fsdp'), may hold values from -0.25 to 0.25
- w_key: bfloat16 [2, 576, 192], P('section', 'fsdp'), may hold values from -0.25 to 0.25
- w_value: bfloat16 [2, 576, 192], P('section', 'fsdp'), may hold values from -0.25 to 0.25
- w_out: bfloat16 [2, 576, 576], P('section', 'fsdp'), may hold values from -2 to 2
- norm_mid: float32 [2, 576], P('section'), may hold values from 0.5 to 1.5
- w_gate: bfloat16 [2, 576, 1536], P('section', 'fsdp'), may hold values from -0.25 to 0.25
- w_up: bfloat16 [2, 576, 1536], P('section', 'fsdp'), may hold values from -0.25 to 0.25
- w_down: bfloat16 [2, 1536, 576], P('section', 'fsdp'), may hold values from -0.15625 to 0.15625
Outputs:
- layer_out: bfloat16 [2, 1, 4, 512, 576], P('section', None, 'fsdp', 'ctx')
- grad_in: float32 [2, 1, 4, 512, 576], P('section', None, 'fsdp', 'ctx')
- grad_norm_in: float32 [2, 576], P('section', 'fsdp')
- grad_query: float32 [2, 576, 576], P('section', 'fsdp')
- grad_key: float32 [2, 576, 192], P('section', 'fsdp')
- grad_value: float32 [2, 576, 192], P('section', 'fsdp')
- grad_out: float32 [2, 576, 576], P('section', 'fsdp')
- grad_norm_mid: float32 [2, 576], P('section', 'fsdp')
- grad_gate: float32 [2, 576, 1536], P('section', 'fsdp')
- grad_up: float32 [2, 576, 1536], P('section', 'fsdp')
- grad_down: float32 [2, 1536, 576], P('section', 'fsdp')
Inputs may be any that keep to these rules, and one draw needn't show every extreme that they name: The rows of every sequence are stored span after span: index c of ctx holds span span_order[2 c] then span span_order[2 c + 1], each of 64 consecutive positions; every span appears once, and the two spans of one index are i and (the number of spans) - 1 - i for some i. `rope_ids`: A token's position minus that of the first token of its packed document; documents follow one another without gaps; the first sequence of every micro-batch is a single document.
All inputs are finite; a program needn't handle non-finite values.
Results may differ from a plain program's by a relative error of at most 0.023.
Values may be sent and summed in bfloat16 or wider, within the bound.
A program may use at most 128 MiB of HBM per device.

v0:
```python
import math

import jax
import jax.numpy as jnp
from jax import lax
from jax.sharding import PartitionSpec as P

KV_HEADS = 3
HEAD = 64


EPS = 1e-05
THETA = 100000.0


def shifted(array, axis, by):
    devices = lax.axis_size(axis)
    pairs = [(i, i + by) for i in range(devices) if 0 <= i + by < devices]
    return lax.ppermute(array, axis, pairs)


def rope_tables(rope_rows):
    half_width = HEAD // 2
    frequency = THETA ** (-jnp.arange(half_width, dtype=jnp.float32) * (2.0 / HEAD))
    angle = rope_rows.astype(jnp.float32)[:, None] * frequency[None, :]
    return (jnp.cos(angle), jnp.sin(angle))


def rotate(vectors, cosine, sine):
    half_width = vectors.shape[-1] // 2
    front = vectors[..., :half_width]
    second = vectors[..., half_width:]
    cos_rows = cosine[:, None, :]
    sin_rows = sine[:, None, :]
    return jnp.concatenate(
        [front * cos_rows - second * sin_rows, second * cos_rows + front * sin_rows], axis=-1
    )


def normalize(field):
    factor = lax.rsqrt(jnp.mean(field * field, axis=-1, keepdims=True) + EPS)
    return (field * factor, factor)


def norm_back(grad_rows, normed, factor, gain):
    scaled = grad_rows * gain
    back = factor * (scaled - normed * jnp.mean(scaled * normed, axis=-1, keepdims=True))
    return (back, jnp.sum(grad_rows * normed, axis=0))


def block_size(row_count):
    return math.gcd(row_count, 512)


def positions_of(span_table, first_row, row_count, shard_rows):
    span_rows = shard_rows // 2
    slot_ids = jnp.arange(span_table.shape[0], dtype=jnp.int32)
    row_ids = first_row + jnp.arange(row_count, dtype=jnp.int32)
    slot_of = 2 * (row_ids // shard_rows) + row_ids % shard_rows // span_rows
    picked = jnp.sum(
        jnp.where(slot_of[:, None] == slot_ids[None, :], span_table[None, :], 0), axis=1
    )
    return picked * span_rows + row_ids % span_rows


def attend_forward(queries, kv_local, span_table, local_pos, shard_rows):
    kv_width = kv_local.shape[1] // 2
    score_scale = HEAD ** (-0.5)
    gathered = lax.all_gather(kv_local, "ctx", axis=0, tiled=True)
    total_rows = gathered.shape[0]
    block_rows = block_size(total_rows)
    block_count = total_rows // block_rows
    key_pos = positions_of(span_table, 0, total_rows, shard_rows).reshape(block_count, block_rows)
    blocks = gathered.reshape(block_count, block_rows, gathered.shape[1])

    def masked_scores(kv_block, block_pos):
        key_heads = kv_block[:, :kv_width].reshape(block_rows, KV_HEADS, HEAD)
        scores = (
            jnp.einsum("rkgd,lkd->rkgl", queries, key_heads, preferred_element_type=jnp.float32)
            * score_scale
        )
        allowed = block_pos[None, :] <= local_pos[:, None]
        return jnp.where(allowed[:, None, None, :], scores, -math.inf)

    def total_pass(running, block_item):
        row_top, row_total = running
        scores = masked_scores(block_item[0], block_item[1])
        new_top = jnp.maximum(row_top, jnp.max(scores, axis=-1))
        anchor = jnp.where(new_top == -math.inf, 0.0, new_top)
        row_total = row_total * jnp.exp(row_top - anchor) + jnp.sum(
            jnp.exp(scores - anchor[..., None]), axis=-1
        )
        return ((new_top, row_total), None)

    initial = (
        jnp.full(queries.shape[:3], -math.inf, jnp.float32),
        jnp.zeros(queries.shape[:3], jnp.float32),
    )
    (row_top, row_total), unused = lax.scan(total_pass, initial, (blocks, key_pos))
    log_total = row_top + jnp.log(row_total)

    def value_pass(summed, block_item):
        kv_block, block_pos = block_item
        scores = masked_scores(kv_block, block_pos)
        value_heads = kv_block[:, kv_width:].reshape(block_rows, KV_HEADS, HEAD)
        probs = jnp.exp(scores - log_total[..., None]).astype(jnp.bfloat16)
        summed = summed + jnp.einsum(
            "rkgl,lkd->rkgd", probs, value_heads, preferred_element_type=jnp.float32
        )
        return (summed, None)

    summed, unused = lax.scan(value_pass, jnp.zeros(queries.shape, jnp.float32), (blocks, key_pos))
    return (summed.astype(jnp.bfloat16), log_total)


def attend_backward(
    queries, kv_local, span_table, local_pos, log_total, grad_att, row_delta, shard_rows
):
    kv_width = kv_local.shape[1] // 2
    score_scale = HEAD ** (-0.5)
    gathered = lax.all_gather(kv_local, "ctx", axis=0, tiled=True)
    total_rows = gathered.shape[0]
    block_rows = block_size(total_rows)
    block_count = total_rows // block_rows
    key_pos = positions_of(span_table, 0, total_rows, shard_rows).reshape(block_count, block_rows)
    blocks = gathered.reshape(block_count, block_rows, gathered.shape[1])

    def backward_block(grad_q, block_item):
        kv_block, block_pos = block_item
        key_heads = kv_block[:, :kv_width].reshape(block_rows, KV_HEADS, HEAD)
        value_heads = kv_block[:, kv_width:].reshape(block_rows, KV_HEADS, HEAD)
        scores = (
            jnp.einsum("rkgd,lkd->rkgl", queries, key_heads, preferred_element_type=jnp.float32)
            * score_scale
        )
        allowed = block_pos[None, :] <= local_pos[:, None]
        scores = jnp.where(allowed[:, None, None, :], scores, -math.inf)
        probs = jnp.exp(scores - log_total[..., None])
        grad_v = jnp.einsum(
            "rkgl,rkgd->lkd",
            probs.astype(jnp.bfloat16),
            grad_att,
            preferred_element_type=jnp.float32,
        )
        grad_p = jnp.einsum(
            "rkgd,lkd->rkgl", grad_att, value_heads, preferred_element_type=jnp.float32
        )
        grad_s = (probs * (grad_p - row_delta[..., None])).astype(jnp.bfloat16)
        grad_q = (
            grad_q
            + jnp.einsum("rkgl,lkd->rkgd", grad_s, key_heads, preferred_element_type=jnp.float32)
            * score_scale
        )
        grad_k = (
            jnp.einsum("rkgl,rkgd->lkd", grad_s, queries, preferred_element_type=jnp.float32)
            * score_scale
        )
        joined = jnp.concatenate(
            [grad_k.reshape(block_rows, kv_width), grad_v.reshape(block_rows, kv_width)], axis=1
        )
        return (grad_q, joined)

    grad_q, pieces = lax.scan(
        backward_block, jnp.zeros(queries.shape, jnp.float32), (blocks, key_pos)
    )
    own_grads = lax.psum_scatter(
        pieces.reshape(total_rows, 2 * kv_width), "ctx", scatter_dimension=0, tiled=True
    )
    return (grad_q, own_grads)


def forward_layer(layer_input, rope_rows, params, span_table, local_pos, shard_rows):
    gain_in, w_q, w_k, w_v, w_o, gain_mid, w_g, w_u, w_d = params
    length = layer_input.shape[0]
    residual = layer_input.astype(jnp.float32)
    normed_in, scale_in = normalize(residual)
    hidden_in = (normed_in * gain_in).astype(jnp.bfloat16)
    cosine, sine = rope_tables(rope_rows)
    query = jnp.dot(hidden_in, w_q, preferred_element_type=jnp.float32).reshape(length, -1, HEAD)
    key_proj = jnp.dot(hidden_in, w_k, preferred_element_type=jnp.float32).reshape(
        length, KV_HEADS, HEAD
    )
    value = jnp.dot(hidden_in, w_v, preferred_element_type=jnp.float32).astype(jnp.bfloat16)
    query_b = rotate(query, cosine, sine).astype(jnp.bfloat16).reshape(length, KV_HEADS, -1, HEAD)
    key_b = rotate(key_proj, cosine, sine).astype(jnp.bfloat16).reshape(length, KV_HEADS * HEAD)
    kv_local = jnp.concatenate([key_b, value], axis=1)
    attended, log_total = attend_forward(query_b, kv_local, span_table, local_pos, shard_rows)
    attended_flat = attended.reshape(length, -1)
    residual_mid = residual + jnp.dot(attended_flat, w_o, preferred_element_type=jnp.float32)
    normed_mid, scale_mid = normalize(residual_mid)
    hidden_mid = (normed_mid * gain_mid).astype(jnp.bfloat16)
    gate_pre = jnp.dot(hidden_mid, w_g, preferred_element_type=jnp.float32)
    up_pre = jnp.dot(hidden_mid, w_u, preferred_element_type=jnp.float32)
    active = (jax.nn.silu(gate_pre) * up_pre).astype(jnp.bfloat16)
    result = residual_mid + jnp.dot(active, w_d, preferred_element_type=jnp.float32)
    saved = (
        normed_in,
        scale_in,
        hidden_in,
        cosine,
        sine,
        query_b,
        kv_local,
        attended,
        log_total,
        normed_mid,
        scale_mid,
        hidden_mid,
        gate_pre,
        up_pre,
        active,
    )
    return (result, saved)


def backward_layer(saved, params, grad_y, span_table, local_pos, shard_rows):
    gain_in, w_q, w_k, w_v, w_o, gain_mid, w_g, w_u, w_d = params
    (
        normed_in,
        scale_in,
        hidden_in,
        cosine,
        sine,
        query_b,
        kv_local,
        attended,
        log_total,
        normed_mid,
        scale_mid,
        hidden_mid,
        gate_pre,
        up_pre,
        active,
    ) = saved
    length = grad_y.shape[0]
    grad_yb = grad_y.astype(jnp.bfloat16)
    grad_wd = jnp.dot(active.T, grad_yb, preferred_element_type=jnp.float32)
    grad_act = jnp.dot(grad_yb, w_d.T, preferred_element_type=jnp.float32)
    sigmoid_gate = jax.nn.sigmoid(gate_pre)
    grad_gate = (grad_act * up_pre * sigmoid_gate * (1.0 + gate_pre * (1.0 - sigmoid_gate))).astype(
        jnp.bfloat16
    )
    grad_up = (grad_act * gate_pre * sigmoid_gate).astype(jnp.bfloat16)
    grad_wg = jnp.dot(hidden_mid.T, grad_gate, preferred_element_type=jnp.float32)
    grad_wu = jnp.dot(hidden_mid.T, grad_up, preferred_element_type=jnp.float32)
    grad_hmid = jnp.dot(grad_gate, w_g.T, preferred_element_type=jnp.float32) + jnp.dot(
        grad_up, w_u.T, preferred_element_type=jnp.float32
    )
    back_mid, grad_gmid = norm_back(grad_hmid, normed_mid, scale_mid, gain_mid)
    grad_mid = grad_y + back_mid
    grad_midb = grad_mid.astype(jnp.bfloat16)
    attended_flat = attended.reshape(length, -1)
    grad_wo = jnp.dot(attended_flat.T, grad_midb, preferred_element_type=jnp.float32)
    grad_att = (
        jnp.dot(grad_midb, w_o.T, preferred_element_type=jnp.float32)
        .astype(jnp.bfloat16)
        .reshape(attended.shape)
    )
    row_delta = jnp.sum(grad_att.astype(jnp.float32) * attended.astype(jnp.float32), axis=-1)
    grad_q, grad_kv = attend_backward(
        query_b, kv_local, span_table, local_pos, log_total, grad_att, row_delta, shard_rows
    )
    kv_width = kv_local.shape[1] // 2
    grad_qraw = (
        rotate(grad_q.reshape(length, -1, HEAD), cosine, -sine)
        .astype(jnp.bfloat16)
        .reshape(length, -1)
    )
    grad_kraw = (
        rotate(grad_kv[:, :kv_width].reshape(length, KV_HEADS, HEAD), cosine, -sine)
        .astype(jnp.bfloat16)
        .reshape(length, kv_width)
    )
    grad_vb = grad_kv[:, kv_width:].astype(jnp.bfloat16)
    grad_wq = jnp.dot(hidden_in.T, grad_qraw, preferred_element_type=jnp.float32)
    grad_wk = jnp.dot(hidden_in.T, grad_kraw, preferred_element_type=jnp.float32)
    grad_wv = jnp.dot(hidden_in.T, grad_vb, preferred_element_type=jnp.float32)
    grad_hin = (
        jnp.dot(grad_qraw, w_q.T, preferred_element_type=jnp.float32)
        + jnp.dot(grad_kraw, w_k.T, preferred_element_type=jnp.float32)
        + jnp.dot(grad_vb, w_v.T, preferred_element_type=jnp.float32)
    )
    back_in, grad_gin = norm_back(grad_hin, normed_in, scale_in, gain_in)
    grad_entry = grad_mid + back_in
    return (
        grad_entry,
        (grad_gin, grad_wq, grad_wk, grad_wv, grad_wo, grad_gmid, grad_wg, grad_wu, grad_wd),
    )


def body(
    block_input,
    cotangent,
    span_order,
    rope_ids,
    norm_in,
    w_query,
    w_key,
    w_value,
    w_out,
    norm_mid,
    w_gate,
    w_up,
    w_down,
):
    micro_count = block_input.shape[0]
    shard_rows = block_input.shape[2]
    ctx_place = lax.axis_index("ctx")
    leading = lax.axis_index("section") == 0
    local_pos = positions_of(span_order, ctx_place * shard_rows, shard_rows, shard_rows)
    gathered = (
        lax.all_gather(w_query[0], "fsdp", axis=0, tiled=True),
        lax.all_gather(w_key[0], "fsdp", axis=0, tiled=True),
        lax.all_gather(w_value[0], "fsdp", axis=0, tiled=True),
        lax.all_gather(w_out[0], "fsdp", axis=0, tiled=True),
        lax.all_gather(w_gate[0], "fsdp", axis=0, tiled=True),
        lax.all_gather(w_up[0], "fsdp", axis=0, tiled=True),
        lax.all_gather(w_down[0], "fsdp", axis=0, tiled=True),
    )
    params = (
        norm_in[0],
        gathered[0],
        gathered[1],
        gathered[2],
        gathered[3],
        norm_mid[0],
        gathered[4],
        gathered[5],
        gathered[6],
    )
    received = jnp.zeros(block_input.shape[2:], jnp.bfloat16)
    kept_states = []
    outputs = []
    for tick_index in range(micro_count + 1):
        fresh_rows = block_input[min(tick_index, micro_count - 1), 0]
        layer_input = jnp.where(leading, fresh_rows, received)
        rope_rows = jnp.where(
            leading,
            rope_ids[min(tick_index, micro_count - 1), 0],
            rope_ids[max(tick_index - 1, 0), 0],
        )
        result, saved = forward_layer(
            layer_input, rope_rows, params, span_order, local_pos, shard_rows
        )
        sent_rows = result.astype(jnp.bfloat16)
        kept_states.append(saved)
        outputs.append(sent_rows)
        if tick_index < micro_count:
            received = shifted(sent_rows, "section", 1)
    regathered = (
        lax.all_gather(w_query[0], "fsdp", axis=0, tiled=True),
        lax.all_gather(w_key[0], "fsdp", axis=0, tiled=True),
        lax.all_gather(w_value[0], "fsdp", axis=0, tiled=True),
        lax.all_gather(w_out[0], "fsdp", axis=0, tiled=True),
        lax.all_gather(w_gate[0], "fsdp", axis=0, tiled=True),
        lax.all_gather(w_up[0], "fsdp", axis=0, tiled=True),
        lax.all_gather(w_down[0], "fsdp", axis=0, tiled=True),
    )
    params_back = (
        norm_in[0],
        regathered[0],
        regathered[1],
        regathered[2],
        regathered[3],
        norm_mid[0],
        regathered[4],
        regathered[5],
        regathered[6],
    )
    returned = jnp.zeros(block_input.shape[2:], jnp.bfloat16)
    grad_sums = None
    grad_inputs = []
    for tick_index in range(micro_count + 1):
        if tick_index < micro_count:
            fresh_rows = cotangent[tick_index, 0]
        else:
            fresh_rows = jnp.zeros_like(cotangent[0, 0])
        arrival = jnp.where(leading, returned, fresh_rows).astype(jnp.float32)
        saved = jax.tree.map(
            lambda left, right: jnp.where(leading, left, right),
            kept_states[max(tick_index - 1, 0)],
            kept_states[min(tick_index + 1, micro_count)],
        )
        grad_entry, terms = backward_layer(
            saved, params_back, arrival, span_order, local_pos, shard_rows
        )
        if grad_sums is None:
            grad_sums = terms
        else:
            grad_sums = jax.tree.map(lambda left, right: left + right, grad_sums, terms)
        grad_inputs.append(grad_entry)
        if tick_index < micro_count:
            returned = shifted(grad_entry.astype(jnp.bfloat16), "section", -1)
    layer_out = jnp.stack([jnp.where(leading, outputs[0], outputs[1])])
    grad_in = jnp.stack([jnp.where(leading, grad_inputs[1], grad_inputs[0])])
    layer_out = layer_out.reshape((1, micro_count, 1) + layer_out.shape[1:])
    grad_in = grad_in.reshape((1, micro_count, 1) + grad_in.shape[1:])
    shares = (
        lax.psum_scatter(grad_sums[0], "fsdp", scatter_dimension=0, tiled=True),
        lax.psum_scatter(grad_sums[1], "fsdp", scatter_dimension=0, tiled=True),
        lax.psum_scatter(grad_sums[2], "fsdp", scatter_dimension=0, tiled=True),
        lax.psum_scatter(grad_sums[3], "fsdp", scatter_dimension=0, tiled=True),
        lax.psum_scatter(grad_sums[4], "fsdp", scatter_dimension=0, tiled=True),
        lax.psum_scatter(grad_sums[5], "fsdp", scatter_dimension=0, tiled=True),
        lax.psum_scatter(grad_sums[6], "fsdp", scatter_dimension=0, tiled=True),
        lax.psum_scatter(grad_sums[7], "fsdp", scatter_dimension=0, tiled=True),
        lax.psum_scatter(grad_sums[8], "fsdp", scatter_dimension=0, tiled=True),
    )
    totals = lax.psum(
        (
            shares[0],
            shares[1],
            shares[2],
            shares[3],
            shares[4],
            shares[5],
            shares[6],
            shares[7],
            shares[8],
        ),
        "ctx",
    )
    return (layer_out, grad_in) + tuple((summed_part[None] for summed_part in totals))


def solution(mesh):
    placed = (
        P(None, "fsdp", "ctx", None),
        P(None, "fsdp", "ctx", None),
        P(),
        P(None, "fsdp", "ctx"),
        P("section", None),
        P("section", "fsdp", None),
        P("section", "fsdp", None),
        P("section", "fsdp", None),
        P("section", "fsdp", None),
        P("section", None),
        P("section", "fsdp", None),
        P("section", "fsdp", None),
        P("section", "fsdp", None),
    )
    return jax.shard_map(
        body,
        mesh=mesh,
        in_specs=placed,
        out_specs=(
            P("section", None, "fsdp", "ctx", None),
            P("section", None, "fsdp", "ctx", None),
            P("section", "fsdp"),
            P("section", "fsdp", None),
            P("section", "fsdp", None),
            P("section", "fsdp", None),
            P("section", "fsdp", None),
            P("section", "fsdp"),
            P("section", "fsdp", None),
            P("section", "fsdp", None),
            P("section", "fsdp", None),
        ),
        check_vma=False,
    )
```

profile of v0, /device:TPU:11, one launch (start us, length us, event | category | flops | bytes accessed | tf_op | source)
XLA Modules:
  0.0 663.0 jit_solution(4798871493568730933)
XLA Ops:
  9.5 7.1 %all-gather.1 = bf16[1,576,192]{2,1,0:T(8,128)(2,1)S(1)} all-gather(bf16[1,144,192]{2,1,0:T(8,128)(2,1)} %param.20), channel_id=3, replica_groups=mesh['section'=2,'ctx'=4,'fsdp'=4] {'fsdp'}, dimensions={1}, use_global_device_ids=true | all-gather | bytes 276480 | tf_op jit(solution)/shard_map/all_gather | solution.py:314
  17.8 9.9 %all-gather = bf16[1,576,192]{2,1,0:T(8,128)(2,1)S(1)} all-gather(bf16[1,144,192]{2,1,0:T(8,128)(2,1)} %param.19), channel_id=2, replica_groups=mesh['section'=2,'ctx'=4,'fsdp'=4] {'fsdp'}, dimensions={1}, use_global_device_ids=true | all-gather | bytes 276480 | tf_op jit(solution)/shard_map/all_gather | solution.py:313
  29.5 12.8 %all_gather.40 = bf16[512,384]{0,1:T(8,128)(2,1)S(1)} all-gather(bf16[128,384]{0,1:T(8,128)(2,1)S(1)} %pad_maximum_fusion.6), channel_id=1, replica_groups=mesh['section'=2,'ctx'=4,'fsdp'=4] {'ctx'}, dimensions={0}, use_global_device_ids=true | all-gather | bytes 491520 | tf_op jit(solution)/shard_map/all_gather | solution.py:69
  42.5 9.6 %all-gather.2 = bf16[1,576,576]{2,1,0:T(8,128)(2,1)S(1)} all-gather(bf16[1,144,576]{2,1,0:T(8,128)(2,1)S(1)} %copy-done.85), channel_id=4, replica_groups=mesh['section'=2,'ctx'=4,'fsdp'=4] {'fsdp'}, dimensions={1}, use_global_device_ids=true | all-gather | bytes 829440 | tf_op jit(solution)/shard_map/all_gather | solution.py:312
  53.2 12.4 %all-gather.3 = bf16[1,576,576]{2,1,0:T(8,128)(2,1)S(1)} all-gather(bf16[1,144,576]{2,1,0:T(8,128)(2,1)S(1)} %copy-done.86), channel_id=5, replica_groups=mesh['section'=2,'ctx'=4,'fsdp'=4] {'fsdp'}, dimensions={1}, use_global_device_ids=true | all-gather | bytes 829440 | tf_op jit(solution)/shard_map/all_gather | solution.py:315
  70.2 11.9 %all-gather.13.cloned.1.call-done = bf16[1,576,1536]{2,1,0:T(8,128)(2,1)} async-done(((bf16[1,144,1536]{2,1,0:T(8,128)(2,1)}), bf16[1,576,1536]{2,1,0:T(8,128)(2,1)}) %all-gather.13.cloned.1.call-update) | async-done | bytes 1769488 | tf_op jit(solution)/shard_map/all_gather | solution.py:317
  82.0 3.0 multiply_convert_fusion.5
  85.0 31.3 %all-gather.15.cloned.1.call-done = bf16[1,1536,576]{1,2,0:T(8,128)(2,1)} async-done(((bf16[1,384,576]{1,2,0:T(8,128)(2,1)}), bf16[1,1536,576]{1,2,0:T(8,128)(2,1)}) %all-gather.15.cloned.1.call-update) | async-done | bytes 1769488 | tf_op jit(solution)/shard_map/all_gather | solution.py:318
  124.0 12.0 %all_gather.46 = bf16[512,384]{0,1:T(8,128)(2,1)S(1)} all-gather(bf16[128,384]{0,1:T(8,128)(2,1)S(1)} %get-tuple-element.211), channel_id=1, replica_groups=mesh['section'=2,'ctx'=4,'fsdp'=4] {'ctx'}, dimensions={0}, use_global_device_ids=true | all-gather | bytes 491520 | tf_op jit(solution)/shard_map/all_gather | solution.py:69
  145.9 11.9 %all_gather.47 = bf16[512,384]{0,1:T(8,128)(2,1)S(1)} all-gather(bf16[128,384]{0,1:T(8,128)(2,1)S(1)} %get-tuple-element.210), channel_id=1, replica_groups=mesh['section'=2,'ctx'=4,'fsdp'=4] {'ctx'}, dimensions={0}, use_global_device_ids=true | all-gather | bytes 491520 | tf_op jit(solution)/shard_map/all_gather | solution.py:121
  167.7 18.9 %reduce-scatter.14.cloned.1.call-done = f32[128,384]{0,1:T(8,128)} async-done(((f32[512,384]{0,1:T(8,128)}), f32[128,384]{0,1:T(8,128)}) %reduce-scatter.14.cloned.1.call-update) | async-done | bytes 196624 | tf_op jit(solution)/shard_map/reduce_scatter | solution.py:166
  192.6 3.0 collective-permute-start.1
  207.0 21.6 %reduce-scatter.16.cloned.1.call-done = f32[128,384]{0,1:T(8,128)} async-done(((f32[512,384]{0,1:T(8,128)}), f32[128,384]{0,1:T(8,128)}) %reduce-scatter.16.cloned.1.call-update) | async-done | bytes 196624 | tf_op jit(solution)/shard_map/reduce_scatter | solution.py:166
  253.5 4.8 reduce-scatter.18.cloned.1.call-done
  258.3 28.8 %reduce-scatter.20.cloned.1.call-done = f32[144,192]{1,0:T(8,128)} async-done(((f32[576,192]{1,0:T(8,128)}), f32[144,192]{1,0:T(8,128)}) %reduce-scatter.20.cloned.1.call-update) | async-done | bytes 110608 | tf_op jit(solution)/shard_map/reduce_scatter | solution.py:402
  287.1 33.4 %reduce-scatter.28.cloned.1.call-done = f32[144,576]{1,0:T(8,128)} async-done(((f32[576,576]{1,0:T(8,128)}), f32[144,576]{1,0:T(8,128)}) %reduce-scatter.28.cloned.1.call-update) | async-done | bytes 331792
  320.5 33.6 %reduce-scatter.30.cloned.1.call-done = f32[144,576]{1,0:T(8,128)} async-done(((f32[576,576]{1,0:T(8,128)}), f32[144,576]{1,0:T(8,128)}) %reduce-scatter.30.cloned.1.call-update) | async-done | bytes 331792
  354.1 50.1 %reduce-scatter.22.cloned.1.call-done = f32[144,1536]{1,0:T(8,128)} async-done(((f32[576,1536]{1,0:T(8,128)}), f32[144,1536]{1,0:T(8,128)}) %reduce-scatter.22.cloned.1.call-update) | async-done | bytes 884752 | tf_op jit(solution)/shard_map/reduce_scatter | solution.py:405
  404.2 50.3 %reduce-scatter.24.cloned.1.call-done = f32[144,1536]{1,0:T(8,128)} async-done(((f32[576,1536]{1,0:T(8,128)}), f32[144,1536]{1,0:T(8,128)}) %reduce-scatter.24.cloned.1.call-update) | async-done | bytes 884752 | tf_op jit(solution)/shard_map/reduce_scatter | solution.py:406
  454.6 50.2 %reduce-scatter.26.cloned.1.call-done = f32[384,576]{0,1:T(8,128)} async-done(((f32[1536,576]{0,1:T(8,128)}), f32[384,576]{0,1:T(8,128)}) %reduce-scatter.26.cloned.1.call-update) | async-done | bytes 884752 | tf_op jit(solution)/shard_map/reduce_scatter | solution.py:407
  506.1 2.8 fusion.61
  510.0 6.3 all-reduce.4
  516.4 9.4 %all-reduce.5 = (f32[1,144]{1,0:T(1,128)}, f32[1,144]{1,0:T(1,128)}) all-reduce(f32[1,144]{1,0:T(1,128)S(1)} %bitcast.404, f32[1,144]{1,0:T(1,128)S(1)} %bitcast.405), channel_id=1, replica_groups=mesh['section'=2,'ctx'=4,'fsdp'=4] {'ctx'}, use_global_device_ids=true, to_apply=%region_21.22 | all-reduce | flops 288 | bytes 2304 | tf_op jit(solution)/shard_map/psum | solution.py:409
  526.7 120.2 %all-reduce.9.cloned.1.call-done = (f32[1,144,576]{2,1,0:T(8,128)}, f32[1,144,192]{2,1,0:T(8,128)}, f32[1,144,192]{2,1,0:T(8,128)}, f32[1,144,576]{2,1,0:T(8,128...) async-done(((f32[1,144,576]{2,1,0:T(8,128)}, f32[1,144,192]{2,1,0:T(8,128)}, f32[1,144,192]{2,1,0:T(8,128)}, f32[1,144,576]{2,1,0:T(8,128)}, ...) | async-done | bytes 3538960 | tf_op jit(solution)/shard_map/psum | solution.py:409
  (386 shorter events, 91.3 us)
Async XLA Ops:
  7.2 60.9 %all-gather.11.cloned.1.call-start = ((), (), s32[]{:S(2)}) async-start(), calls=%async_computation.16 | async-start | bytes 2211840 | tf_op jit(solution)/shard_map/all_gather | solution.py:316
  8.0 74.1 %all-gather.13.cloned.1.call-start = ((), (), s32[]{:S(2)}) async-start(), calls=%async_computation.17 | async-start | bytes 2211840 | tf_op jit(solution)/shard_map/all_gather | solution.py:317
  8.7 107.6 %all-gather.15.cloned.1.call-start = ((), (), s32[]{:S(2)}) async-start(), calls=%async_computation.18 | async-start | bytes 2211840 | tf_op jit(solution)/shard_map/all_gather | solution.py:318
  9.4 177.1 %reduce-scatter.14.cloned.1.call-start = ((), (), s32[]{:S(2)}) async-start(), calls=%async_computation.9 | async-start | bytes 983040 | tf_op jit(solution)/shard_map/reduce_scatter | solution.py:166
  17.8 34.8 %copy-start.104 = (f32[128]{0:T(128)}, f32[128]{0:T(128)S(1)}, u32[]{:S(2)}) copy-start(f32[128]{0:T(128)S(1)} %fusion.85) | copy-start | bytes 1540
  27.9 95.4 %copy-start.78 = (f32[576]{0:T(1024)}, f32[576]{0:T(1024)S(1)}, u32[]{:S(2)}) copy-start(f32[576]{0:T(1024)S(1)} %reduce) | copy-start | bytes 6916
  53.2 84.1 %copy-start.37 = (pred[128,512]{0,1:T(8,128)(4,1)}, pred[128,512]{0,1:T(8,128)(4,1)S(1)}, u32[]{:S(2)}) copy-start(pred[128,512]{0,1:T(8,128)(4,1)S(1)} %broadcast_compare_fusion) | copy-start | bytes 196612
  65.7 92.4 %copy-start.2 = (bf16[1,576,576]{2,1,0:T(8,128)(2,1)}, bf16[1,576,576]{2,1,0:T(8,128)(2,1)S(1)}, u32[]{:S(2)}) copy-start(bf16[1,576,576]{2,1,0:T(8,128)(2,1)S(1)} %all-gather.3) | copy-start | bytes 1990660
  65.7 92.1 %copy-start.80 = (f32[576]{0:T(1024)}, f32[576]{0:T(1024)S(1)}, u32[]{:S(2)}) copy-start(f32[576]{0:T(1024)S(1)} %reduce.1) | copy-start | bytes 6916
  85.0 34.8 %copy-start.26 = (bf16[128,1536]{1,0:T(8,128)(2,1)}, bf16[128,1536]{1,0:T(8,128)(2,1)S(1)}, u32[]{:S(2)}) copy-start(bf16[128,1536]{1,0:T(8,128)(2,1)S(1)} %get-tuple-element.223) | copy-start | bytes 1179652
  118.5 3.3 collective-permute-start
  163.4 65.2 %reduce-scatter.16.cloned.1.call-start = ((), (), s32[]{:S(2)}) async-start(), calls=%async_computation.10 | async-start | bytes 983040 | tf_op jit(solution)/shard_map/reduce_scatter | solution.py:166
  192.6 4.0 collective-permute-start.1
  206.3 52.0 %reduce-scatter.18.cloned.1.call-start = ((), (), s32[]{:S(2)}) async-start(), calls=%async_computation.11 | async-start | bytes 737280 | tf_op jit(solution)/shard_map/reduce_scatter | solution.py:401
  230.7 56.4 %reduce-scatter.20.cloned.1.call-start = ((), (), s32[]{:S(2)}) async-start(), calls=%async_computation.12 | async-start | bytes 737280 | tf_op jit(solution)/shard_map/reduce_scatter | solution.py:402
  236.3 84.1 %reduce-scatter.28.cloned.1.call-start = ((), (), s32[]{:S(2)}) async-start(), calls=%async_computation.19 | async-start | bytes 1843200
  239.3 114.8 %reduce-scatter.30.cloned.1.call-start = ((), (), s32[]{:S(2)}) async-start(), calls=%async_computation.20 | async-start | bytes 1843200
  241.8 162.4 %reduce-scatter.22.cloned.1.call-start = ((), (), s32[]{:S(2)}) async-start(), calls=%async_computation.13 | async-start | bytes 4423680 | tf_op jit(solution)/shard_map/reduce_scatter | solution.py:405
  245.2 209.4 %reduce-scatter.24.cloned.1.call-start = ((), (), s32[]{:S(2)}) async-start(), calls=%async_computation.14 | async-start | bytes 4423680 | tf_op jit(solution)/shard_map/reduce_scatter | solution.py:406
  249.2 255.5 %reduce-scatter.26.cloned.1.call-start = ((), (), s32[]{:S(2)}) async-start(), calls=%async_computation.15 | async-start | bytes 4423680 | tf_op jit(solution)/shard_map/reduce_scatter | solution.py:407
  253.4 251.4 %copy-start.112 = (u32[32]{0:T(128)S(1)}, u32[32]{0:T(128)}, u32[]{:S(2)}) copy-start(u32[32]{0:T(128)} %constant.248) | copy-start | bytes 388
  253.4 252.6 %copy-start.20 = (f32[128,576]{0,1:T(8,128)S(1)}, f32[128,576]{0,1:T(8,128)}, u32[]{:S(2)}) copy-start(f32[128,576]{0,1:T(8,128)} %copy-done.19) | copy-start | bytes 884740
  253.4 252.6 %copy-start.63 = (bf16[128,576]{0,1:T(8,128)(2,1)S(1)}, bf16[128,576]{0,1:T(8,128)(2,1)}, u32[]{:S(2)}) copy-start(bf16[128,576]{0,1:T(8,128)(2,1)} %copy-done.62) | copy-start | bytes 442372
  253.4 393.5 %all-reduce.9.cloned.1.call-start = ((), (), s32[]{:S(2)}) async-start(), calls=%async_computation.21 | async-start | bytes 7372800 | tf_op jit(solution)/shard_map/psum | solution.py:409
  (105 other events, 753.8 us)
Sparse Core Ops, SparseCore 0:
  9.9 35.3 all-gather.10
  47.1 34.9 all-gather.12
  83.9 32.4 all-gather.14
  163.5 23.0 reduce-scatter.13
  206.4 22.1 reduce-scatter.15
  231.9 26.3 reduce-scatter.17
  262.0 25.0 reduce-scatter.19
  290.0 30.3 reduce-scatter.27
  323.7 30.3 reduce-scatter.29
  357.0 47.1 reduce-scatter.21
  407.3 47.2 reduce-scatter.23
  457.5 47.2 reduce-scatter.25
  507.7 139.1 all-reduce.8
where the time goes:
time: 668 us; the launch traced here: 663 us
  waiting for transfers between devices  460 us (69%)
  blocking collectives  91.5 us (14%)
  matrix products  55.3 us (8%)
  local copies, waits for them, and re-layouts  22.7 us (3%)
  between operations  16.3 us (2%)
  other arithmetic  11.9 us (2%)
    psum x1, waiting for transfers between devices, body(): lax.psum((shares[0], shares[1], shares[2], shares[3], shares[4], shares[5...  120 us
    unnamed x15, waiting for transfers between devices  69.2 us
    reduce_scatter x1, waiting for transfers between devices, body(): lax.psum_scatter(grad_sums[7], 'fsdp', scatter_dimension=0, tiled=True)  50.3 us
    reduce_scatter x1, waiting for transfers between devices, body(): lax.psum_scatter(grad_sums[8], 'fsdp', scatter_dimension=0, tiled=True)  50.2 us
    reduce_scatter x1, waiting for transfers between devices, body(): lax.psum_scatter(grad_sums[6], 'fsdp', scatter_dimension=0, tiled=True)  50.1 us
    reduce_scatter x2, waiting for transfers between devices, attend_backward(): lax.psum_scatter(pieces.reshape(total_rows, 2 * kv_width), 'ctx', scatter...  40.5 us
    all_gather x1, waiting for transfers between devices, body(): lax.all_gather(w_down[0], 'fsdp', axis=0, tiled=True)  31.3 us
    reduce_scatter x1, waiting for transfers between devices, body(): lax.psum_scatter(grad_sums[3], 'fsdp', scatter_dimension=0, tiled=True)  28.8 us
  transfers between devices with their start and end apart: 15, of which 14 were waited for; matrix products, arithmetic and copies ran while one was open for 6% of the time, Pallas kernels for 0%

commit v1 on v0

--- a/solution.py
+++ b/solution.py
@@ -1,8 +1,11 @@
+import functools
 import math
 
 import jax
 import jax.numpy as jnp
 from jax import lax
+from jax.experimental import pallas as pl
+from jax.experimental.pallas import tpu as pltpu
 from jax.sharding import PartitionSpec as P
 
 KV_HEADS = 3
@@ -11,6 +14,321 @@
 
 EPS = 1e-05
 THETA = 100000.0
+
+
+LANES = 128
+VMEM_BYTES = 48 * 1024 * 1024
+
+
+def padded(width):
+    return -(-width // LANES) * LANES
+
+
+def greet(peers):
+    barrier = pltpu.get_barrier_semaphore()
+    for axis, place in peers:
+        pl.semaphore_signal(
+            barrier, inc=1, device_id={axis: place}, device_id_type=pl.DeviceIdType.MESH
+        )
+    pl.semaphore_wait(barrier, len(peers))
+
+
+def push(source, target, send_sem, recv_sem, axis, place):
+    return pltpu.make_async_remote_copy(
+        src_ref=source,
+        dst_ref=target,
+        send_sem=send_sem,
+        recv_sem=recv_sem,
+        device_id={axis: place},
+        device_id_type=pl.DeviceIdType.MESH,
+    )
+
+
+def call_options(collective_id):
+    return pltpu.CompilerParams(
+        collective_id=collective_id, has_side_effects=True, vmem_limit_bytes=VMEM_BYTES
+    )
+
+
+def spread_kernel(count, own_ref, all_ref, send_sem, recv_sem):
+    me = lax.axis_index("ctx")
+    greet([("ctx", lax.rem(me + step, count)) for step in range(1, count)])
+    copies = []
+    for step in range(1, count):
+        copy = push(
+            own_ref,
+            all_ref.at[me],
+            send_sem.at[step - 1],
+            recv_sem.at[step - 1],
+            "ctx",
+            lax.rem(me + step, count),
+        )
+        copy.start()
+        copies.append(copy)
+    all_ref[me] = own_ref[...]
+    for copy in copies:
+        copy.wait()
+
+
+def spread(own, collective_id):
+    count = lax.axis_size("ctx")
+    whole = pl.BlockSpec(memory_space=pltpu.VMEM)
+    return pl.pallas_call(
+        functools.partial(spread_kernel, count),
+        out_shape=jax.ShapeDtypeStruct((count,) + own.shape, own.dtype),
+        in_specs=[whole],
+        out_specs=whole,
+        scratch_shapes=[
+            pltpu.SemaphoreType.DMA((count - 1,)),
+            pltpu.SemaphoreType.DMA((count - 1,)),
+        ],
+        compiler_params=call_options(collective_id),
+        name="spread",
+    )(own).reshape((count * own.shape[0],) + own.shape[1:])
+
+
+def collect_kernel(count, pieces_ref, sum_ref, packed, landed, send_sem, recv_sem):
+    me = lax.axis_index("ctx")
+    greet([("ctx", lax.rem(me + step, count)) for step in range(1, count)])
+    copies = []
+    for step in range(1, count):
+        place = lax.rem(me + step, count)
+        packed[step - 1] = pieces_ref[place].astype(jnp.bfloat16)
+        copy = push(
+            packed.at[step - 1],
+            landed.at[step - 1],
+            send_sem.at[step - 1],
+            recv_sem.at[step - 1],
+            "ctx",
+            place,
+        )
+        copy.start()
+        copies.append(copy)
+    total = pieces_ref[me]
+    for step, copy in enumerate(copies):
+        copy.wait_recv()
+        total = total + landed[step].astype(jnp.float32)
+    sum_ref[...] = total
+    for copy in copies:
+        copy.wait_send()
+
+
+def collect(pieces, collective_id):
+    count = lax.axis_size("ctx")
+    whole = pl.BlockSpec(memory_space=pltpu.VMEM)
+    blocks = pieces.reshape((count, -1) + pieces.shape[1:])
+    slots = (count - 1,) + blocks.shape[1:]
+    return pl.pallas_call(
+        functools.partial(collect_kernel, count),
+        out_shape=jax.ShapeDtypeStruct(blocks.shape[1:], jnp.float32),
+        in_specs=[whole],
+        out_specs=whole,
+        scratch_shapes=[
+            pltpu.VMEM(slots, jnp.bfloat16),
+            pltpu.VMEM(slots, jnp.bfloat16),
+            pltpu.SemaphoreType.DMA((count - 1,)),
+            pltpu.SemaphoreType.DMA((count - 1,)),
+        ],
+        compiler_params=call_options(collective_id),
+        name="collect",
+    )(blocks)
+
+
+def grads_kernel(
+    active,
+    rows_f,
+    count_c,
+    part,
+    products,
+    hid_in,
+    att,
+    hid_mid,
+    grad_y,
+    d_qkv,
+    d_mid,
+    d_ff,
+    act,
+    gains,
+    out,
+    made,
+    landed,
+    summed,
+    landed_c,
+    total,
+    send_f,
+    recv_f,
+    send_c,
+    recv_c,
+    send_g,
+    recv_g,
+):
+    off_ff, off_down, off_gain, off_out, off_qkv, end = products
+    f_place = lax.axis_index("fsdp")
+    c_place = lax.axis_index("ctx")
+
+    def put(block, offset, left, right):
+        width = right.shape[1]
+        for first in range(0, width, 512):
+            size = min(512, width - first)
+            made[block, :, pl.ds(offset + first, size)] = jnp.dot(
+                left, right[:, first : first + size], preferred_element_type=jnp.float32
+            ).astype(jnp.bfloat16)
+
+    def compute(block):
+        put(block, off_ff, hid_mid[block], d_ff[...])
+        step_rows = act.shape[2]
+        for index in range(rows_f):
+            put(block, off_down + index * step_rows, grad_y[index], act[block])
+        made[block, :, pl.ds(off_gain, LANES)] = gains[block]
+        put(block, off_out, att[block], d_mid[...])
+        put(block, off_qkv, hid_in[block], d_qkv[...])
+        if end < count_c * part:
+            made[block, :, pl.ds(end, count_c * part - end)] = jnp.zeros(
+                (made.shape[1], count_c * part - end), jnp.bfloat16
+            )
+
+    def columns(index):
+        return pl.ds(pl.multiple_of(index * part, LANES), part)
+
+    @pl.when(lax.axis_index("section") == active)
+    def run():
+        f_peers = [lax.rem(f_place + step, rows_f) for step in range(1, rows_f)]
+        c_peers = [lax.rem(c_place + step, count_c) for step in range(1, count_c)]
+        greet([("fsdp", place) for place in f_peers] + [("ctx", place) for place in c_peers])
+        order = c_peers + [c_place]
+        copies_f = []
+        for step, place in enumerate(f_peers):
+            compute(place)
+            row = []
+            for index, part_place in enumerate(order):
+                copy = push(
+                    made.at[place, :, columns(part_place)],
+                    landed.at[step, :, columns(part_place)],
+                    send_f.at[step, index],
+                    recv_f.at[step, index],
+                    "fsdp",
+                    place,
+                )
+                copy.start()
+                row.append(copy)
+            copies_f.append(row)
+        compute(f_place)
+        copies_c = []
+        for index, part_place in enumerate(order):
+            here = columns(part_place)
+            value = made[f_place, :, here].astype(jnp.float32)
+            for step in range(rows_f - 1):
+                copies_f[step][index].wait_recv()
+                value = value + landed[step, :, here].astype(jnp.float32)
+            if index < count_c - 1:
+                summed[index] = value.astype(jnp.bfloat16)
+                copy = push(
+                    summed.at[index],
+                    landed_c.at[index],
+                    send_c.at[index],
+                    recv_c.at[index],
+                    "ctx",
+                    part_place,
+                )
+                copy.start()
+                copies_c.append(copy)
+            else:
+                total[...] = value
+        value = total[...]
+        for index, copy in enumerate(copies_c):
+            copy.wait_recv()
+            value = value + landed_c[index].astype(jnp.float32)
+        mine = columns(c_place)
+        out[:, mine] = value.astype(jnp.bfloat16)
+        copies_g = []
+        for index, place in enumerate(c_peers):
+            copy = push(
+                out.at[:, mine],
+                out.at[:, mine],
+                send_g.at[index],
+                recv_g.at[index],
+                "ctx",
+                place,
+            )
+            copy.start()
+            copies_g.append(copy)
+        for copy in copies_g:
+            copy.wait()
+        for copy in copies_c:
+            copy.wait_send()
+        for row in copies_f:
+            for copy in row:
+                copy.wait_send()
+
+
+def padded_columns(array):
+    return jnp.pad(array, ((0, 0), (0, padded(array.shape[1]) - array.shape[1])))
+
+
+def reduce_grads(active, operands, collective_id):
+    hid_in, d_qkv, att, d_mid, hid_mid, d_ff, act, grad_y, gain_in, gain_mid = operands
+    rows_f = lax.axis_size("fsdp")
+    count_c = lax.axis_size("ctx")
+    tokens, features = hid_in.shape
+    rows = features // rows_f
+    assert att.shape == hid_in.shape
+
+    def turned(array):
+        return array.T.reshape(rows_f, rows, tokens)
+
+    act_cols = act.shape[1] // rows_f
+    act_blocks = act.reshape(tokens, rows_f, act_cols).transpose(1, 0, 2)
+    gains = jnp.stack([gain_in, gain_mid], axis=-1).reshape(rows_f, rows, 2)
+    gains = jnp.pad(gains, ((0, 0), (0, 0), (0, LANES - 2))).astype(jnp.bfloat16)
+    d_mid = padded_columns(d_mid)
+    d_qkv = padded_columns(d_qkv)
+    off_ff = 0
+    off_down = off_ff + d_ff.shape[1]
+    off_gain = off_down + act.shape[1]
+    off_out = off_gain + LANES
+    off_qkv = off_out + d_mid.shape[1]
+    end = off_qkv + d_qkv.shape[1]
+    part = -(-end // (LANES * count_c)) * LANES
+    whole = pl.BlockSpec(memory_space=pltpu.VMEM)
+    out = pl.pallas_call(
+        functools.partial(
+            grads_kernel,
+            active,
+            rows_f,
+            count_c,
+            part,
+            (off_ff, off_down, off_gain, off_out, off_qkv, end),
+        ),
+        out_shape=jax.ShapeDtypeStruct((rows, count_c * part), jnp.bfloat16),
+        in_specs=[whole] * 9,
+        out_specs=whole,
+        scratch_shapes=[
+            pltpu.VMEM((rows_f, rows, count_c * part), jnp.bfloat16),
+            pltpu.VMEM((rows_f - 1, rows, count_c * part), jnp.bfloat16),
+            pltpu.VMEM((count_c - 1, rows, part), jnp.bfloat16),
+            pltpu.VMEM((count_c - 1, rows, part), jnp.bfloat16),
+            pltpu.VMEM((rows, part), jnp.float32),
+            pltpu.SemaphoreType.DMA((rows_f - 1, count_c)),
+            pltpu.SemaphoreType.DMA((rows_f - 1, count_c)),
+            pltpu.SemaphoreType.DMA((count_c - 1,)),
+            pltpu.SemaphoreType.DMA((count_c - 1,)),
+            pltpu.SemaphoreType.DMA((count_c - 1,)),
+            pltpu.SemaphoreType.DMA((count_c - 1,)),
+        ],
+        compiler_params=call_options(collective_id),
+        name="reduce_grads",
+    )(
+        turned(hid_in),
+        turned(att),
+        turned(hid_mid),
+        turned(grad_y),
+        d_qkv,
+        d_mid,
+        d_ff,
+        act_blocks,
+        gains,
+    )
+    return out, (off_ff, off_down, off_gain, off_out, off_qkv, act_cols)
 
 
 def shifted(array, axis, by):
@@ -63,10 +381,9 @@
     return picked * span_rows + row_ids % span_rows
 
 
-def attend_forward(queries, kv_local, span_table, local_pos, shard_rows):
-    kv_width = kv_local.shape[1] // 2
+def attend_forward(queries, gathered, span_table, local_pos, shard_rows):
+    kv_width = gathered.shape[1] // 2
     score_scale = HEAD ** (-0.5)
-    gathered = lax.all_gather(kv_local, "ctx", axis=0, tiled=True)
     total_rows = gathered.shape[0]
     block_rows = block_size(total_rows)
     block_count = total_rows // block_rows
@@ -114,11 +431,10 @@
 
 
 def attend_backward(
-    queries, kv_local, span_table, local_pos, log_total, grad_att, row_delta, shard_rows
+    queries, gathered, span_table, local_pos, log_total, grad_att, row_delta, shard_rows, call_id
 ):
-    kv_width = kv_local.shape[1] // 2
+    kv_width = gathered.shape[1] // 2
     score_scale = HEAD ** (-0.5)
-    gathered = lax.all_gather(kv_local, "ctx", axis=0, tiled=True)
     total_rows = gathered.shape[0]
     block_rows = block_size(total_rows)
     block_count = total_rows // block_rows
@@ -163,13 +479,11 @@
     grad_q, pieces = lax.scan(
         backward_block, jnp.zeros(queries.shape, jnp.float32), (blocks, key_pos)
     )
-    own_grads = lax.psum_scatter(
-        pieces.reshape(total_rows, 2 * kv_width), "ctx", scatter_dimension=0, tiled=True
-    )
+    own_grads = collect(pieces.reshape(total_rows, 2 * kv_width), call_id)
     return (grad_q, own_grads)
 
 
-def forward_layer(layer_input, rope_rows, params, span_table, local_pos, shard_rows):
+def forward_layer(layer_input, rope_rows, params, span_table, local_pos, shard_rows, call_id):
     gain_in, w_q, w_k, w_v, w_o, gain_mid, w_g, w_u, w_d = params
     length = layer_input.shape[0]
     residual = layer_input.astype(jnp.float32)
@@ -183,7 +497,7 @@
     value = jnp.dot(hidden_in, w_v, preferred_element_type=jnp.float32).astype(jnp.bfloat16)
     query_b = rotate(query, cosine, sine).astype(jnp.bfloat16).reshape(length, KV_HEADS, -1, HEAD)
     key_b = rotate(key_proj, cosine, sine).astype(jnp.bfloat16).reshape(length, KV_HEADS * HEAD)
-    kv_local = jnp.concatenate([key_b, value], axis=1)
+    kv_local = spread(jnp.concatenate([key_b, value], axis=1), call_id)
     attended, log_total = attend_forward(query_b, kv_local, span_table, local_pos, shard_rows)
     attended_flat = attended.reshape(length, -1)
     residual_mid = residual + jnp.dot(attended_flat, w_o, preferred_element_type=jnp.float32)
@@ -213,7 +527,7 @@
     return (result, saved)
 
 
-def backward_layer(saved, params, grad_y, span_table, local_pos, shard_rows):
+def backward_layer(saved, params, grad_y, span_table, local_pos, shard_rows, call_id):
     gain_in, w_q, w_k, w_v, w_o, gain_mid, w_g, w_u, w_d = params
     (
         normed_in,
@@ -234,15 +548,12 @@
     ) = saved
     length = grad_y.shape[0]
     grad_yb = grad_y.astype(jnp.bfloat16)
-    grad_wd = jnp.dot(active.T, grad_yb, preferred_element_type=jnp.float32)
     grad_act = jnp.dot(grad_yb, w_d.T, preferred_element_type=jnp.float32)
     sigmoid_gate = jax.nn.sigmoid(gate_pre)
     grad_gate = (grad_act * up_pre * sigmoid_gate * (1.0 + gate_pre * (1.0 - sigmoid_gate))).astype(
         jnp.bfloat16
     )
     grad_up = (grad_act * gate_pre * sigmoid_gate).astype(jnp.bfloat16)
-    grad_wg = jnp.dot(hidden_mid.T, grad_gate, preferred_element_type=jnp.float32)
-    grad_wu = jnp.dot(hidden_mid.T, grad_up, preferred_element_type=jnp.float32)
     grad_hmid = jnp.dot(grad_gate, w_g.T, preferred_element_type=jnp.float32) + jnp.dot(
         grad_up, w_u.T, preferred_element_type=jnp.float32
     )
@@ -250,7 +561,6 @@
     grad_mid = grad_y + back_mid
     grad_midb = grad_mid.astype(jnp.bfloat16)
     attended_flat = attended.reshape(length, -1)
-    grad_wo = jnp.dot(attended_flat.T, grad_midb, preferred_element_type=jnp.float32)
     grad_att = (
         jnp.dot(grad_midb, w_o.T, preferred_element_type=jnp.float32)
         .astype(jnp.bfloat16)
@@ -258,7 +568,7 @@
     )
     row_delta = jnp.sum(grad_att.astype(jnp.float32) * attended.astype(jnp.float32), axis=-1)
     grad_q, grad_kv = attend_backward(
-        query_b, kv_local, span_table, local_pos, log_total, grad_att, row_delta, shard_rows
+        query_b, kv_local, span_table, local_pos, log_total, grad_att, row_delta, shard_rows, call_id
     )
     kv_width = kv_local.shape[1] // 2
     grad_qraw = (
@@ -272,9 +582,6 @@
         .reshape(length, kv_width)
     )
     grad_vb = grad_kv[:, kv_width:].astype(jnp.bfloat16)
-    grad_wq = jnp.dot(hidden_in.T, grad_qraw, preferred_element_type=jnp.float32)
-    grad_wk = jnp.dot(hidden_in.T, grad_kraw, preferred_element_type=jnp.float32)
-    grad_wv = jnp.dot(hidden_in.T, grad_vb, preferred_element_type=jnp.float32)
     grad_hin = (
         jnp.dot(grad_qraw, w_q.T, preferred_element_type=jnp.float32)
         + jnp.dot(grad_kraw, w_k.T, preferred_element_type=jnp.float32)
@@ -284,7 +591,18 @@
     grad_entry = grad_mid + back_in
     return (
         grad_entry,
-        (grad_gin, grad_wq, grad_wk, grad_wv, grad_wo, grad_gmid, grad_wg, grad_wu, grad_wd),
+        (
+            hidden_in,
+            jnp.concatenate([grad_qraw, grad_kraw, grad_vb], axis=1),
+            attended_flat,
+            grad_midb,
+            hidden_mid,
+            jnp.concatenate([grad_gate, grad_up], axis=1),
+            active,
+            grad_yb,
+            grad_gin,
+            grad_gmid,
+        ),
     )
 
 
@@ -340,35 +658,15 @@
             rope_ids[max(tick_index - 1, 0), 0],
         )
         result, saved = forward_layer(
-            layer_input, rope_rows, params, span_order, local_pos, shard_rows
+            layer_input, rope_rows, params, span_order, local_pos, shard_rows, tick_index
         )
         sent_rows = result.astype(jnp.bfloat16)
         kept_states.append(saved)
         outputs.append(sent_rows)
         if tick_index < micro_count:
             received = shifted(sent_rows, "section", 1)
-    regathered = (
-        lax.all_gather(w_query[0], "fsdp", axis=0, tiled=True),
-        lax.all_gather(w_key[0], "fsdp", axis=0, tiled=True),
-        lax.all_gather(w_value[0], "fsdp", axis=0, tiled=True),
-        lax.all_gather(w_out[0], "fsdp", axis=0, tiled=True),
-        lax.all_gather(w_gate[0], "fsdp", axis=0, tiled=True),
-        lax.all_gather(w_up[0], "fsdp", axis=0, tiled=True),
-        lax.all_gather(w_down[0], "fsdp", axis=0, tiled=True),
-    )
-    params_back = (
-        norm_in[0],
-        regathered[0],
-        regathered[1],
-        regathered[2],
-        regathered[3],
-        norm_mid[0],
-        regathered[4],
-        regathered[5],
-        regathered[6],
-    )
     returned = jnp.zeros(block_input.shape[2:], jnp.bfloat16)
-    grad_sums = None
+    reduced = []
     grad_inputs = []
     for tick_index in range(micro_count + 1):
         if tick_index < micro_count:
@@ -382,43 +680,38 @@
             kept_states[min(tick_index + 1, micro_count)],
         )
         grad_entry, terms = backward_layer(
-            saved, params_back, arrival, span_order, local_pos, shard_rows
-        )
-        if grad_sums is None:
-            grad_sums = terms
-        else:
-            grad_sums = jax.tree.map(lambda left, right: left + right, grad_sums, terms)
+            saved, params, arrival, span_order, local_pos, shard_rows, 2 + tick_index
+        )
         grad_inputs.append(grad_entry)
         if tick_index < micro_count:
             returned = shifted(grad_entry.astype(jnp.bfloat16), "section", -1)
+        share, places = reduce_grads(1 - tick_index, terms, 4 + tick_index)
+        reduced.append(share)
     layer_out = jnp.stack([jnp.where(leading, outputs[0], outputs[1])])
     grad_in = jnp.stack([jnp.where(leading, grad_inputs[1], grad_inputs[0])])
     layer_out = layer_out.reshape((1, micro_count, 1) + layer_out.shape[1:])
     grad_in = grad_in.reshape((1, micro_count, 1) + grad_in.shape[1:])
-    shares = (
-        lax.psum_scatter(grad_sums[0], "fsdp", scatter_dimension=0, tiled=True),
-        lax.psum_scatter(grad_sums[1], "fsdp", scatter_dimension=0, tiled=True),
-        lax.psum_scatter(grad_sums[2], "fsdp", scatter_dimension=0, tiled=True),
-        lax.psum_scatter(grad_sums[3], "fsdp", scatter_dimension=0, tiled=True),
-        lax.psum_scatter(grad_sums[4], "fsdp", scatter_dimension=0, tiled=True),
-        lax.psum_scatter(grad_sums[5], "fsdp", scatter_dimension=0, tiled=True),
-        lax.psum_scatter(grad_sums[6], "fsdp", scatter_dimension=0, tiled=True),
-        lax.psum_scatter(grad_sums[7], "fsdp", scatter_dimension=0, tiled=True),
-        lax.psum_scatter(grad_sums[8], "fsdp", scatter_dimension=0, tiled=True),
-    )
-    totals = lax.psum(
-        (
-            shares[0],
-            shares[1],
-            shares[2],
-            shares[3],
-            shares[4],
-            shares[5],
-            shares[6],
-            shares[7],
-            shares[8],
-        ),
-        "ctx",
+    share = jnp.where(leading, reduced[1], reduced[0]).astype(jnp.float32)
+    off_ff, off_down, off_gain, off_out, off_qkv, act_cols = places
+
+    def cut(first, width):
+        return share[:, first : first + width]
+
+    q_width, kv_width, ff_width = w_query.shape[2], w_key.shape[2], w_gate.shape[2]
+    rows = share.shape[0]
+    down_parts = block_input.shape[3] // rows
+    grad_down = cut(off_down, down_parts * act_cols).reshape(rows, down_parts, act_cols)
+    grad_down = grad_down.transpose(2, 1, 0).reshape(act_cols, down_parts * rows)
+    totals = (
+        cut(off_gain, 1)[:, 0],
+        cut(off_qkv, q_width),
+        cut(off_qkv + q_width, kv_width),
+        cut(off_qkv + q_width + kv_width, kv_width),
+        cut(off_out, block_input.shape[3]),
+        cut(off_gain + 1, 1)[:, 0],
+        cut(off_ff, ff_width),
+        cut(off_ff + ff_width, ff_width),
+        grad_down,
     )
     return (layer_out, grad_in) + tuple((summed_part[None] for summed_part in totals))
 

time: 668 us -> 353 us (0.53)
  waiting for transfers between devices: 460 us -> 41.3 us
  Pallas kernels: 0 us -> 126 us
  blocking collectives: 91.5 us -> 40.2 us
  local copies, waits for them, and re-layouts: 22.7 us -> 52.2 us
  matrix products: 55.3 us -> 38.9 us
  starting transfers between devices: 5.08 us -> 18.9 us
  other arithmetic: 11.9 us -> 19.7 us
    reduce_scatter x7 -> x0, waiting for transfers between devices: 225 us -> none  [the longest x1 50.3 us: body(): lax.psum_scatter(grad_sums[7], 'fsdp', scatter_dimension=0, tiled=True)]
    pallas_call x0 -> x6, Pallas kernels: none -> 126 us  [the longest x2 74.9 us: reduce_grads(): pl.pallas_call(functools.partial(grads_kernel, active, rows_f, count_c, p...]
    psum x1 -> x0, waiting for transfers between devices: 120 us -> none  [body(): lax.psum((shares[0], shares[1], shares[2], shares[3], shares[4], shares[5...]
    unnamed x15 -> x3, waiting for transfers between devices: 69.2 us -> 2.06 us
    all_gather x3 -> x0, blocking collectives: 36.7 us -> none  [the longest x2 24.8 us: attend_forward(): gathered = lax.all_gather(kv_local, 'ctx', axis=0, tiled=True)]
    dot_general x14 -> x0, matrix products: 19.3 us -> none  [the longest x2 3.97 us: backward_layer(): jnp.dot(hidden_in.T, grad_qraw, preferred_element_type=jnp.float32)]
    ppermute x2, starting transfers between devices: 4.33 us -> 18.8 us  [shifted(): return lax.ppermute(array, axis, pairs)]
    concatenate x0 -> x8, local copies, waits for them, and re-layouts: none -> 11 us  [backward_block(): jnp.concatenate([grad_k.reshape(block_rows, kv_width), grad_v.reshape(blo...]
  transfers between devices with their start and end apart: 15 -> 5, of which waited for: 14 -> 2; matrix products, arithmetic and copies ran while one was open for 6% -> 8% of each run, Pallas kernels for 0% -> 23%
where the time goes in v1:
time: 353 us
  Pallas kernels  126 us (36%)
  local copies, waits for them, and re-layouts  52.2 us (15%)
  waiting for transfers between devices  41.3 us (12%)
  blocking collectives  40.2 us (11%)
  matrix products  38.9 us (11%)
  other arithmetic  19.7 us (6%)
  starting transfers between devices  18.9 us (5%)
  between operations  15.6 us (4%)
    pallas_call x2, Pallas kernels, reduce_grads(): pl.pallas_call(functools.partial(grads_kernel, active, rows_f, count_c, p...  74.9 us
    all_gather x1, waiting for transfers between devices, body(): lax.all_gather(w_down[0], 'fsdp', axis=0, tiled=True)  31.1 us
    pallas_call x2, Pallas kernels, collect(): pl.pallas_call(functools.partial(collect_kernel, count), out_shape=jax.Sh...  30.9 us
    pallas_call x2, Pallas kernels, spread(): pl.pallas_call(functools.partial(spread_kernel, count), out_shape=jax.Sha...  20.2 us
    ppermute x2, starting transfers between devices, shifted(): return lax.ppermute(array, axis, pairs)  18.8 us
    all_gather x1, blocking collectives, body(): lax.all_gather(w_out[0], 'fsdp', axis=0, tiled=True)  14.1 us
    unnamed x210, local copies, waits for them, and re-layouts  13.5 us
    concatenate x8, local copies, waits for them, and re-layouts, backward_block(): jnp.concatenate([grad_k.reshape(block_rows, kv_width), grad_v.reshape(blo...  11 us
  transfers between devices with their start and end apart: 5, of which 2 were waited for; matrix products, arithmetic and copies ran while one was open for 8% of the time, Pallas kernels for 23%

profile of v1, /device:TPU:11, one launch (start us, length us, event | category | flops | bytes accessed | tf_op | source)
XLA Modules:
  0.0 352.7 jit_solution(18418533883476051122)
XLA Ops:
  12.9 7.1 %all-gather = bf16[1,576,192]{2,1,0:T(8,128)(2,1)S(1)} all-gather(bf16[1,144,192]{2,1,0:T(8,128)(2,1)} %param.19), channel_id=2, replica_groups=mesh['section'=2,'ctx'=4,'fsdp'=4] {'fsdp'}, dimensions={1}, use_global_device_ids=true | all-gather | bytes 276480 | tf_op jit(solution)/shard_map/all_gather | solution.py:631
  21.4 7.9 %all-gather.1 = bf16[1,576,192]{2,1,0:T(8,128)(2,1)S(1)} all-gather(bf16[1,144,192]{2,1,0:T(8,128)(2,1)S(1)} %copy-done.75), channel_id=3, replica_groups=mesh['section'=2,'ctx'=4,'fsdp'=4] {'fsdp'}, dimensions={1}, use_global_device_ids=true | all-gather | bytes 276480 | tf_op jit(solution)/shard_map/all_gather | solution.py:632
  29.9 8.1 %spread.2 = bf16[4,128,384]{2,1,0:T(8,128)(2,1)S(1)} custom-call(bf16[128,384]{1,0:T(8,128)(2,1)S(1)} %pad_maximum_fusion.8.own_ref), custom_call_target="tpu_custom_call" | custom-call | tf_op jit(solution)/shard_map/spread/pallas_call | solution.py:76
  38.8 11.0 %all-gather.2 = bf16[1,576,576]{2,1,0:T(8,128)(2,1)S(1)} all-gather(bf16[1,144,576]{2,1,0:T(8,128)(2,1)S(1)} %copy-done.74), channel_id=4, replica_groups=mesh['section'=2,'ctx'=4,'fsdp'=4] {'fsdp'}, dimensions={1}, use_global_device_ids=true | all-gather | bytes 829440 | tf_op jit(solution)/shard_map/all_gather | solution.py:630
  50.8 14.1 %all-gather.3 = bf16[1,576,576]{2,1,0:T(8,128)(2,1)S(1)} all-gather(bf16[1,144,576]{2,1,0:T(8,128)(2,1)} %param.21), channel_id=5, replica_groups=mesh['section'=2,'ctx'=4,'fsdp'=4] {'fsdp'}, dimensions={1}, use_global_device_ids=true | all-gather | bytes 829440 | tf_op jit(solution)/shard_map/all_gather | solution.py:633
  66.2 1.8 copy.273
  72.3 2.9 fusion.30
  75.1 8.1 %all-gather.13.cloned.1.call-done = bf16[1,576,1536]{2,1,0:T(8,128)(2,1)} async-done(((bf16[1,144,1536]{2,1,0:T(8,128)(2,1)}), bf16[1,576,1536]{2,1,0:T(8,128)(2,1)}) %all-gather.13.cloned.1.call-update) | async-done | bytes 1769488 | tf_op jit(solution)/shard_map/all_gather | solution.py:635
  83.2 3.2 multiply_convert_fusion.5
  86.4 31.1 %all-gather.15.cloned.1.call-done = bf16[1,1536,576]{1,2,0:T(8,128)(2,1)} async-done(((bf16[1,384,576]{1,2,0:T(8,128)(2,1)}), bf16[1,1536,576]{1,2,0:T(8,128)(2,1)}) %all-gather.15.cloned.1.call-update) | async-done | bytes 1769488 | tf_op jit(solution)/shard_map/all_gather | solution.py:636
  117.5 2.4 fusion.55
  128.0 12.1 %spread.3 = bf16[4,128,384]{2,1,0:T(8,128)(2,1)S(1)} custom-call(bf16[128,384]{1,0:T(8,128)(2,1)S(1)} %pad_maximum_fusion.9.own_ref), custom_call_target="tpu_custom_call" | custom-call | tf_op jit(solution)/shard_map/spread/pallas_call | solution.py:76
  165.8 9.9 %collect.2 = f32[128,384]{1,0:T(8,128)S(1)} custom-call(f32[4,128,384]{2,1,0:T(8,128)S(1)} %pad_maximum_fusion.pieces_ref), custom_call_target="tpu_custom_call" | custom-call | tf_op jit(solution)/shard_map/collect/pallas_call | solution.py:121
  177.4 2.0 fusion.147
  179.4 17.2 %collective-permute-start.1 = (bf16[128,576]{1,0:T(8,128)(2,1)}, bf16[128,576]{1,0:T(8,128)(2,1)}, u32[]{:S(2)}, u32[]{:S(2)}) collective-permute-start(bf16[128,576]{1,0:T(8,128)(2,1)} %fusion.147), channel_id=1, source_target_pairs={{16,0},{17,1},{18,2},{19,3},{20,4},{21,5},{22,6},{23,7},{24,8},{25... | collective-permute-start | bytes 442376 | tf_op jit(solution)/shard_map/ppermute | solution.py:337
  196.7 2.4 fusion.63
  205.0 74.6 %reduce_grads.3 = bf16[144,6656]{1,0:T(8,128)(2,1)S(1)} custom-call(bf16[4,144,128]{2,1,0:T(8,128)(2,1)S(1)} %bitcast.372, bf16[4,144,128]{2,1,0:T(8,128)(2,1)S(1)} %bitcast.370, bf16[4,144,128]{2,1,0:T(8,128)(2,1)S(1)} %bitcast.374, bf16[4,144,128]{2,1,0:T(8,128)(2,1)S(1)} %bitcast.376, bf16[128,1024]{1,0:T(8,128)(2,1)S(1)} %fusion.104.d_qkv, ...), custom_call_target="tpu_custom_call" | custom-call | tf_op jit(solution)/shard_map/reduce_grads/pallas_call | solution.py:293
  279.7 2.4 multiply_convert_fusion.1
  291.9 1.9 concatenate.99
  293.8 1.9 concatenate.98
  295.7 2.0 copy.305
  297.7 2.0 copy.306
  301.1 21.0 %collect.3 = f32[128,384]{1,0:T(8,128)S(1)} custom-call(f32[4,128,384]{2,1,0:T(8,128)S(1)} %pad_maximum_fusion.1.pieces_ref), custom_call_target="tpu_custom_call" | custom-call | tf_op jit(solution)/shard_map/collect/pallas_call | solution.py:121
  331.1 2.1 multiply_reduce_fusion.3
  (371 shorter events, 88.0 us)
Async XLA Ops:
  7.2 65.0 %all-gather.11.cloned.1.call-start = ((), (), s32[]{:S(2)}) async-start(), calls=%async_computation | async-start | bytes 2211840 | tf_op jit(solution)/shard_map/all_gather | solution.py:634
  7.9 75.3 %all-gather.13.cloned.1.call-start = ((), (), s32[]{:S(2)}) async-start(), calls=%async_computation.1 | async-start | bytes 2211840 | tf_op jit(solution)/shard_map/all_gather | solution.py:635
  8.7 108.8 %all-gather.15.cloned.1.call-start = ((), (), s32[]{:S(2)}) async-start(), calls=%async_computation.2 | async-start | bytes 2211840 | tf_op jit(solution)/shard_map/all_gather | solution.py:636
  12.7 164.7 %copy-start.16 = (bf16[1,1,128,576]{3,2,1,0:T(8,128)(2,1)}, bf16[1,1,128,576]{3,2,1,0:T(8,128)(2,1)S(1)}, u32[]{:S(2)}) copy-start(bf16[1,1,128,576]{3,2,1,0:T(8,128)(2,1)S(1)} %copy.266) | copy-start | bytes 442372
  12.9 37.3 %copy-start.81 = (f32[128]{0:T(128)}, f32[128]{0:T(128)S(1)}, u32[]{:S(2)}) copy-start(f32[128]{0:T(128)S(1)} %add_rsqrt_fusion.3) | copy-start | bytes 1540
  20.0 105.9 %copy-start.24 = (bf16[1,576,192]{2,1,0:T(8,128)(2,1)}, bf16[1,576,192]{2,1,0:T(8,128)(2,1)S(1)}, u32[]{:S(2)}) copy-start(bf16[1,576,192]{2,1,0:T(8,128)(2,1)S(1)} %all-gather) | copy-start | bytes 663556
  20.2 106.9 %copy-start.63 = (f32[576]{0:T(1024)}, f32[576]{0:T(1024)S(1)}, u32[]{:S(2)}) copy-start(f32[576]{0:T(1024)S(1)} %reduce) | copy-start | bytes 6916
  29.3 96.3 %copy-start.30 = (bf16[1,576,192]{2,1,0:T(8,128)(2,1)}, bf16[1,576,192]{2,1,0:T(8,128)(2,1)S(1)}, u32[]{:S(2)}) copy-start(bf16[1,576,192]{2,1,0:T(8,128)(2,1)S(1)} %all-gather.1) | copy-start | bytes 663556
  38.8 26.1 %copy-start.94 = (f32[1,576]{1,0:T(1,128)S(1)}, f32[1,576]{1,0:T(1,128)}, u32[]{:S(2)}) copy-start(f32[1,576]{1,0:T(1,128)} %param.22) | copy-start | bytes 6916
  49.8 126.1 %copy-start.12 = (bf16[1,576,576]{2,1,0:T(8,128)(2,1)}, bf16[1,576,576]{2,1,0:T(8,128)(2,1)S(1)}, u32[]{:S(2)}) copy-start(bf16[1,576,576]{2,1,0:T(8,128)(2,1)S(1)} %all-gather.2) | copy-start | bytes 1990660
  64.9 91.6 %copy-start.14 = (bf16[1,576,576]{2,1,0:T(8,128)(2,1)}, bf16[1,576,576]{2,1,0:T(8,128)(2,1)S(1)}, u32[]{:S(2)}) copy-start(bf16[1,576,576]{2,1,0:T(8,128)(2,1)S(1)} %all-gather.3) | copy-start | bytes 1990660
  65.0 90.7 %copy-start.70 = (f32[576]{0:T(1024)}, f32[576]{0:T(1024)S(1)}, u32[]{:S(2)}) copy-start(f32[576]{0:T(1024)S(1)} %reduce.1) | copy-start | bytes 6916
  66.2 55.2 %copy-start.40 = (bf16[1,1,128,576]{3,2,1,0:T(8,128)(2,1)}, bf16[1,1,128,576]{3,2,1,0:T(8,128)(2,1)S(1)}, u32[]{:S(2)}) copy-start(bf16[1,1,128,576]{3,2,1,0:T(8,128)(2,1)S(1)} %copy.286) | copy-start | bytes 442372
  86.4 38.5 %copy-start.102 = (f32[128]{0:T(128)S(1)}, f32[128]{0:T(128)}, u32[]{:S(2)}) copy-start(f32[128]{0:T(128)} %copy-done.101) | copy-start | bytes 1540
  119.9 3.9 %collective-permute-start = (bf16[128,576]{1,0:T(8,128)(2,1)S(1)}, bf16[128,576]{1,0:T(8,128)(2,1)}, u32[]{:S(2)}, u32[]{:S(2)}) collective-permute-start(bf16[128,576]{1,0:T(8,128)(2,1)S(1)} %fusion.55), channel_id=1, source_target_pairs={{0,16},{1,17},{2,18},{3,19},{4,20},{5,21},{6,22},{7,23},{8,24},{9,... | collective-permute-start | bytes 442376 | tf_op jit(solution)/shard_map/ppermute | solution.py:337
  124.9 52.5 %copy-start.18 = (bf16[128,576]{1,0:T(8,128)(2,1)}, bf16[128,576]{1,0:T(8,128)(2,1)S(1)}, u32[]{:S(2)}) copy-start(bf16[128,576]{1,0:T(8,128)(2,1)S(1)} %get-tuple-element.234) | copy-start | bytes 442372
  179.4 100.3 %collective-permute-start.1 = (bf16[128,576]{1,0:T(8,128)(2,1)}, bf16[128,576]{1,0:T(8,128)(2,1)}, u32[]{:S(2)}, u32[]{:S(2)}) collective-permute-start(bf16[128,576]{1,0:T(8,128)(2,1)} %fusion.147), channel_id=1, source_target_pairs={{16,0},{17,1},{18,2},{19,3},{20,4},{21,5},{22,6},{23,7},{24,8},{25... | collective-permute-start | bytes 442376 | tf_op jit(solution)/shard_map/ppermute | solution.py:337
  199.6 80.0 %copy-start = (bf16[576,128]{1,0:T(8,128)(2,1)}, bf16[576,128]{1,0:T(8,128)(2,1)S(1)}, u32[]{:S(2)}) copy-start(bf16[576,128]{1,0:T(8,128)(2,1)S(1)} %copy.311) | copy-start | bytes 442372
  199.8 79.8 %copy-start.2 = (bf16[576,128]{1,0:T(8,128)(2,1)}, bf16[576,128]{1,0:T(8,128)(2,1)S(1)}, u32[]{:S(2)}) copy-start(bf16[576,128]{1,0:T(8,128)(2,1)S(1)} %copy.312) | copy-start | bytes 442372
  203.0 76.7 %copy-start.33 = (f32[128,1536]{1,0:T(8,128)S(1)}, f32[128,1536]{1,0:T(8,128)}, u32[]{:S(2)}) copy-start(f32[128,1536]{1,0:T(8,128)} %copy-done.32) | copy-start | bytes 2359300
  295.7 27.8 %copy-start.88 = (bf16[576]{0:T(1024)(128)(2,1)S(1)}, bf16[576]{0:T(1024)(128)(2,1)}, u32[]{:S(2)}) copy-start(bf16[576]{0:T(1024)(128)(2,1)} %get-tuple-element.218) | copy-start | bytes 3460
  297.7 30.5 %copy-start.68 = (f32[128,32]{0,1:T(8,128)S(1)}, f32[128,32]{0,1:T(8,128)}, u32[]{:S(2)}) copy-start(f32[128,32]{0,1:T(8,128)} %get-tuple-element.266) | copy-start | bytes 49156
  299.7 31.4 %copy-start.65 = (f32[576]{0:T(1024)S(1)}, f32[576]{0:T(1024)}, u32[]{:S(2)}) copy-start(f32[576]{0:T(1024)} %copy-done.63) | copy-start | bytes 6916
  299.7 31.4 %copy-start.78 = (f32[128]{0:T(128)S(1)}, f32[128]{0:T(128)}, u32[]{:S(2)}) copy-start(f32[128]{0:T(128)} %copy-done.76) | copy-start | bytes 1540
  (84 other events, 511.0 us)
Sparse Core Ops, SparseCore 0:
  9.9 35.7 all-gather.10
  47.5 35.7 all-gather.12
  85.0 32.4 all-gather.14

commit v2 on v1

--- a/solution.py
+++ b/solution.py
@@ -196,22 +196,27 @@
         c_peers = [lax.rem(c_place + step, count_c) for step in range(1, count_c)]
         greet([("fsdp", place) for place in f_peers] + [("ctx", place) for place in c_peers])
         order = c_peers + [c_place]
-        copies_f = []
+        copies_f = [[] for place in f_peers]
+
+        def send_part(step, index):
+            here = columns(order[index])
+            copy = push(
+                made.at[f_peers[step], :, here],
+                landed.at[step, :, here],
+                send_f.at[step, index],
+                recv_f.at[step, index],
+                "fsdp",
+                f_peers[step],
+            )
+            copy.start()
+            copies_f[step].append(copy)
+
         for step, place in enumerate(f_peers):
             compute(place)
-            row = []
-            for index, part_place in enumerate(order):
-                copy = push(
-                    made.at[place, :, columns(part_place)],
-                    landed.at[step, :, columns(part_place)],
-                    send_f.at[step, index],
-                    recv_f.at[step, index],
-                    "fsdp",
-                    place,
-                )
-                copy.start()
-                row.append(copy)
-            copies_f.append(row)
+            send_part(step, 0)
+        for index in range(1, count_c):
+            for step in range(rows_f - 1):
+                send_part(step, index)
         compute(f_place)
         copies_c = []
         for index, part_place in enumerate(order):
@@ -331,6 +336,87 @@
     return out, (off_ff, off_down, off_gain, off_out, off_qkv, act_cols)
 
 
+def weights_kernel(active, number, held, *refs):
+    shards = refs[:number]
+    outs = refs[number * (2 if held else 1) :][:number]
+    send_sem, recv_sem, own_sem = refs[-3:]
+    me = lax.axis_index("fsdp")
+    near = me + 1 - 2 * lax.rem(me, 2)
+    far = lax.rem(me + 2, 4)
+
+    @pl.when(lax.axis_index("section") == active)
+    def run():
+        greet([("fsdp", near), ("fsdp", far)])
+
+        def halves(index):
+            rows = shards[index].shape[0]
+            first = rows // 2 // 16 * 16
+            return pl.ds(0, first), pl.ds(first, rows - first)
+
+        def send(index, slot, source, block, rows, place):
+            copy = push(
+                source,
+                outs[index].at[block, rows],
+                send_sem.at[index, slot],
+                recv_sem.at[index, slot],
+                "fsdp",
+                place,
+            )
+            copy.start()
+            return copy
+
+        copies = []
+        for index in range(number):
+            top, low = halves(index)
+            copies.append(
+                [
+                    send(index, 0, shards[index].at[top], me, top, near),
+                    send(index, 1, shards[index].at[low], me, low, far),
+                    send(index, 2, shards[index].at[low], me, low, near),
+                    send(index, 3, shards[index].at[top], me, top, far),
+                ]
+            )
+        locals_ = []
+        for index in range(number):
+            copy = pltpu.make_async_copy(shards[index], outs[index].at[me], own_sem.at[index])
+            copy.start()
+            locals_.append(copy)
+        for index in range(number):
+            top, low = halves(index)
+            copies[index][0].wait_recv()
+            copies[index].append(send(index, 4, outs[index].at[near, top], near, top, far))
+            copies[index][1].wait_recv()
+            copies[index].append(send(index, 5, outs[index].at[far, low], far, low, near))
+        for index in range(number):
+            for slot in range(2, 6):
+                copies[index][slot].wait_recv()
+            for copy in copies[index]:
+                copy.wait_send()
+            locals_[index].wait()
+
+
+def gather_weights(active, shards, held, collective_id):
+    count = lax.axis_size("fsdp")
+    assert count == 4
+    number = len(shards)
+    anywhere = pl.BlockSpec(memory_space=pl.ANY)
+    operands = tuple(shards) + tuple(held or ())
+    return pl.pallas_call(
+        functools.partial(weights_kernel, active, number, held is not None),
+        out_shape=[jax.ShapeDtypeStruct((count,) + shard.shape, shard.dtype) for shard in shards],
+        in_specs=[anywhere] * len(operands),
+        out_specs=[anywhere] * number,
+        scratch_shapes=[
+            pltpu.SemaphoreType.DMA((number, 6)),
+            pltpu.SemaphoreType.DMA((number, 6)),
+            pltpu.SemaphoreType.DMA((number,)),
+        ],
+        input_output_aliases={number + index: index for index in range(len(held or ()))},
+        compiler_params=call_options(collective_id),
+        name="gather_weights",
+    )(*operands)
+
+
 def shifted(array, axis, by):
     devices = lax.axis_size(axis)
     pairs = [(i, i + by) for i in range(devices) if 0 <= i + by < devices]
@@ -626,26 +712,14 @@
     ctx_place = lax.axis_index("ctx")
     leading = lax.axis_index("section") == 0
     local_pos = positions_of(span_order, ctx_place * shard_rows, shard_rows, shard_rows)
-    gathered = (
-        lax.all_gather(w_query[0], "fsdp", axis=0, tiled=True),
-        lax.all_gather(w_key[0], "fsdp", axis=0, tiled=True),
-        lax.all_gather(w_value[0], "fsdp", axis=0, tiled=True),
-        lax.all_gather(w_out[0], "fsdp", axis=0, tiled=True),
-        lax.all_gather(w_gate[0], "fsdp", axis=0, tiled=True),
-        lax.all_gather(w_up[0], "fsdp", axis=0, tiled=True),
-        lax.all_gather(w_down[0], "fsdp", axis=0, tiled=True),
-    )
-    params = (
-        norm_in[0],
-        gathered[0],
-        gathered[1],
-        gathered[2],
-        gathered[3],
-        norm_mid[0],
-        gathered[4],
-        gathered[5],
-        gathered[6],
-    )
+    shards = (w_query[0], w_key[0], w_value[0], w_out[0], w_gate[0], w_up[0], w_down[0])
+    held = gather_weights(0, shards, None, 6)
+
+    def params_of(blocks):
+        full = [block.reshape((-1, block.shape[2])) for block in blocks]
+        return (norm_in[0], *full[:4], norm_mid[0], *full[4:])
+
+    params = params_of(held)
     received = jnp.zeros(block_input.shape[2:], jnp.bfloat16)
     kept_states = []
     outputs = []
@@ -664,6 +738,10 @@
         kept_states.append(saved)
         outputs.append(sent_rows)
         if tick_index < micro_count:
+            sent_rows, held = lax.optimization_barrier((sent_rows, tuple(held)))
+            held = gather_weights(1, shards, held, 7)
+            sent_rows, held = lax.optimization_barrier((sent_rows, tuple(held)))
+            params = params_of(held)
             received = shifted(sent_rows, "section", 1)
     returned = jnp.zeros(block_input.shape[2:], jnp.bfloat16)
     reduced = []

time: 353 us -> 370 us (1.048)
  local copies, waits for them, and re-layouts: 52.2 us -> 101 us
  waiting for transfers between devices: 41.3 us -> 0.01 us
  blocking collectives: 40.2 us -> 0 us
  Pallas kernels: 126 us -> 159 us
  other arithmetic: 19.7 us -> 40.4 us
  matrix products: 38.9 us -> 53.9 us
  between operations: 15.6 us -> 2.57 us
  starting transfers between devices: 18.9 us -> 9.7 us
    all_gather x4 -> x0, blocking collectives: 40.2 us -> none  [the longest x1 14.1 us: body(): lax.all_gather(w_out[0], 'fsdp', axis=0, tiled=True)]
    all_gather x3 -> x0, waiting for transfers between devices: 39.2 us -> none  [the longest x1 31.1 us: body(): lax.all_gather(w_down[0], 'fsdp', axis=0, tiled=True)]
    pallas_call x0 -> x2, Pallas kernels: none -> 35.4 us  [gather_weights(): pl.pallas_call(functools.partial(weights_kernel, active, number, held is...]
    unnamed x210 -> x299, local copies, waits for them, and re-layouts: 13.5 us -> 35.8 us
    dot_general x2, matrix products: 1.56 us -> 13.9 us  [backward_layer(): jnp.dot(grad_kraw, w_k.T, preferred_element_type=jnp.float32)]
    pallas_call x2, Pallas kernels: 74.9 us -> 85.4 us  [reduce_grads(): pl.pallas_call(functools.partial(grads_kernel, active, rows_f, count_c, p...]
    pallas_call x2, Pallas kernels: 30.9 us -> 20.8 us  [collect(): pl.pallas_call(functools.partial(collect_kernel, count), out_shape=jax.Sh...]
    ppermute x2, starting transfers between devices: 18.8 us -> 9.7 us  [shifted(): return lax.ppermute(array, axis, pairs)]
  transfers between devices with their start and end apart: 5 -> 2, of which waited for: 2 -> 0; matrix products, arithmetic and copies ran while one was open for 8% -> 8% of each run, Pallas kernels for 23% -> 23%
where the time goes in v2:
time: 370 us; the launch traced here: 367 us
  Pallas kernels  159 us (43%)
  local copies, waits for them, and re-layouts  101 us (27%)
  matrix products  53.9 us (15%)
  other arithmetic  40.4 us (11%)
  starting transfers between devices  9.7 us (3%)
    pallas_call x2, Pallas kernels, reduce_grads(): pl.pallas_call(functools.partial(grads_kernel, active, rows_f, count_c, p...  85.4 us
    unnamed x299, local copies, waits for them, and re-layouts  35.8 us
    pallas_call x2, Pallas kernels, gather_weights(): pl.pallas_call(functools.partial(weights_kernel, active, number, held is...  35.4 us
    pallas_call x2, Pallas kernels, collect(): pl.pallas_call(functools.partial(collect_kernel, count), out_shape=jax.Sh...  20.8 us
    pallas_call x2, Pallas kernels, spread(): pl.pallas_call(functools.partial(spread_kernel, count), out_shape=jax.Sha...  17.8 us
    dot_general x2, matrix products, backward_layer(): jnp.dot(grad_kraw, w_k.T, preferred_element_type=jnp.float32)  13.9 us
    concatenate x8, local copies, waits for them, and re-layouts, backward_block(): jnp.concatenate([grad_k.reshape(block_rows, kv_width), grad_v.reshape(blo...  10.3 us
    ppermute x2, starting transfers between devices, shifted(): return lax.ppermute(array, axis, pairs)  9.7 us
  transfers between devices with their start and end apart: 2, of which 0 were waited for; matrix products, arithmetic and copies ran while one was open for 8% of the time, Pallas kernels for 23%

profile of v2, /device:TPU:11, one launch (start us, length us, event | category | flops | bytes accessed | tf_op | source)
XLA Modules:
  0.0 367.0 jit_solution(2776170587991014478)
XLA Ops:
  1.8 2.0 copy.295
  23.7 8.1 %spread.2 = bf16[4,128,384]{2,1,0:T(8,128)(2,1)S(1)} custom-call(bf16[128,384]{1,0:T(8,128)(2,1)S(1)} %pad_maximum_fusion.6.own_ref), custom_call_target="tpu_custom_call" | custom-call | tf_op jit(solution)/shard_map/spread/pallas_call | solution.py:76
  33.5 1.8 copy.300
  37.9 1.8 copy.301
  49.4 2.4 fusion.19
  56.6 34.6 %gather_weights.3 = (bf16[4,144,576]{2,1,0:T(8,128)(2,1)S(1)}, bf16[4,144,192]{2,1,0:T(8,128)(2,1)S(1)}, bf16[4,144,192]{2,1,0:T(8,128)(2,1)S(1)}, bf16[4,144,57...) custom-call(bf16[144,576]{1,0:T(8,128)(2,1)S(1)} %bitcast.365, ...), custom_call_target="tpu_custom_call", output_to_operand_aliasing={{0}: (7, {}), {1}: (8, {}), {2}: (9, {}), {3}: (10, {}), {4... | custom-call | tf_op jit(solution)/shard_map/gather_weights/pallas_call | solution.py:404
  103.4 1.9 convolution_convert_fusion.2
  112.0 9.6 %spread.3 = bf16[4,128,384]{2,1,0:T(8,128)(2,1)S(1)} custom-call(bf16[128,384]{1,0:T(8,128)(2,1)S(1)} %pad_maximum_fusion.7.own_ref), custom_call_target="tpu_custom_call" | custom-call | tf_op jit(solution)/shard_map/spread/pallas_call | solution.py:76
  121.7 1.8 broadcast_select_fusion
  124.4 1.8 copy.311
  126.1 1.7 copy.312
  138.6 1.7 copy.322
  140.4 2.0 select_bitcast_fusion.1
  158.9 1.9 concatenate.90
  160.8 2.0 copy.327
  162.8 1.9 concatenate.89
  164.7 2.0 copy.326
  168.1 6.8 %collect.2 = f32[128,384]{1,0:T(8,128)S(1)} custom-call(f32[4,128,384]{2,1,0:T(8,128)S(1)} %pad_maximum_fusion.pieces_ref), custom_call_target="tpu_custom_call" | custom-call | tf_op jit(solution)/shard_map/collect/pallas_call | solution.py:121
  180.5 13.6 %convolution_add_fusion.4 = f32[128,576]{1,0:T(8,128)S(1)} fusion(f32[128,576]{1,0:T(8,128)S(1)} %fusion.104, bf16[128,192]{0,1:T(8,128)(2,1)S(1)} %bitcast.417, bf16[576,192]{1,0:T(8,128)(2,1)S(1)} %bitcast.342), kind=kOutput, calls=%fused_computation.30 | convolution fusion | flops 28385280 | bytes 860160 | tf_op jit(solution)/shard_map/dot_general | solution.py:673
  196.0 8.2 %collective-permute-start.1 = (bf16[128,576]{1,0:T(8,128)(2,1)}, bf16[128,576]{1,0:T(8,128)(2,1)}, u32[]{:S(2)}, u32[]{:S(2)}) collective-permute-start(bf16[128,576]{1,0:T(8,128)(2,1)} %fusion.89), channel_id=1, source_target_pairs={{16,0},{17,1},{18,2},{19,3},{20,4},{21,5},{22,6},{23,7},{24,8},{25... | collective-permute-start | bytes 442376 | tf_op jit(solution)/shard_map/ppermute | solution.py:423
  218.1 1.9 copy.348
  220.0 1.9 copy.349
  233.9 85.0 %reduce_grads.3 = bf16[144,6656]{1,0:T(8,128)(2,1)S(1)} custom-call(bf16[4,144,128]{2,1,0:T(8,128)(2,1)S(1)} %bitcast.360, bf16[4,144,128]{2,1,0:T(8,128)(2,1)S(1)} %bitcast.354, bf16[4,144,128]{2,1,0:T(8,128)(2,1)S(1)} %bitcast.362, bf16[4,144,128]{2,1,0:T(8,128)(2,1)S(1)} %bitcast.368, bf16[128,1024]{1,0:T(8,128)(2,1)S(1)} %fusion.42.d_qkv, ...), custom_call_target="tpu_custom_call" | custom-call | tf_op jit(solution)/shard_map/reduce_grads/pallas_call | solution.py:298
  332.5 14.1 %collect.3 = f32[128,384]{1,0:T(8,128)S(1)} custom-call(f32[4,128,384]{2,1,0:T(8,128)S(1)} %pad_maximum_fusion.1.pieces_ref), custom_call_target="tpu_custom_call" | custom-call | tf_op jit(solution)/shard_map/collect/pallas_call | solution.py:121
  (451 shorter events, 153.9 us)
Async XLA Ops:
  5.0 13.6 %copy-start.146 = (s32[1,1,128]{2,1,0:T(1,128)S(1)}, s32[1,1,128]{2,1,0:T(1,128)}, u32[]{:S(2)}) copy-start(s32[1,1,128]{2,1,0:T(1,128)} %param.16) | copy-start | bytes 1540
  5.0 13.6 %copy-start.125 = (f32[128]{0:T(128)}, f32[128]{0:T(128)S(1)}, u32[]{:S(2)}) copy-start(f32[128]{0:T(128)S(1)} %add_rsqrt_fusion.3) | copy-start | bytes 1540
  5.7 12.9 %copy-start.104 = (f32[576]{0:T(1024)}, f32[576]{0:T(1024)S(1)}, u32[]{:S(2)}) copy-start(f32[576]{0:T(1024)S(1)} %reduce) | copy-start | bytes 6916
  54.8 36.4 %copy-start.112 = (bf16[128,1536]{1,0:T(8,128)(2,1)}, bf16[128,1536]{1,0:T(8,128)(2,1)S(1)}, u32[]{:S(2)}) copy-start(bf16[128,1536]{1,0:T(8,128)(2,1)S(1)} %get-tuple-element.337) | copy-start | bytes 1179652
  92.0 8.6 %collective-permute-start = (bf16[128,576]{1,0:T(8,128)(2,1)}, bf16[128,576]{1,0:T(8,128)(2,1)}, u32[]{:S(2)}, u32[]{:S(2)}) collective-permute-start(bf16[128,576]{1,0:T(8,128)(2,1)} %fusion.16), channel_id=1, source_target_pairs={{0,16},{1,17},{2,18},{3,19},{4,20},{5,21},{6,22},{7,23},{8,24},{9,... | collective-permute-start | bytes 442376 | tf_op jit(solution)/shard_map/ppermute | solution.py:423
  177.8 16.3 %copy-start.5 = (bf16[4,144,192]{2,1,0:T(8,128)(2,1)S(1)}, bf16[4,144,192]{2,1,0:T(8,128)(2,1)}, u32[]{:S(2)}) copy-start(bf16[4,144,192]{2,1,0:T(8,128)(2,1)} %copy-done.4) | copy-start | bytes 663556
  177.8 16.3 %copy-start.20 = (f32[128,384]{1,0:T(8,128)S(1)}, f32[128,384]{1,0:T(8,128)}, u32[]{:S(2)}) copy-start(f32[128,384]{1,0:T(8,128)} %copy-done.19) | copy-start | bytes 589828
  177.8 16.3 %copy-start.45 = (bf16[1,1,128,576]{3,2,1,0:T(8,128)(2,1)S(1)}, bf16[1,1,128,576]{3,2,1,0:T(8,128)(2,1)}, u32[]{:S(2)}) copy-start(bf16[1,1,128,576]{3,2,1,0:T(8,128)(2,1)} %copy-done.42) | copy-start | bytes 442372
  177.8 16.4 %copy-start.50 = (bf16[128,576]{1,0:T(8,128)(2,1)S(1)}, bf16[128,576]{1,0:T(8,128)(2,1)}, u32[]{:S(2)}) copy-start(bf16[128,576]{1,0:T(8,128)(2,1)} %copy-done.47) | copy-start | bytes 442372
  177.8 16.4 %copy-start.106 = (f32[576]{0:T(1024)S(1)}, f32[576]{0:T(1024)}, u32[]{:S(2)}) copy-start(f32[576]{0:T(1024)} %copy-done.104) | copy-start | bytes 6916
  177.8 16.4 %copy-start.121 = (f32[128]{0:T(128)S(1)}, f32[128]{0:T(128)}, u32[]{:S(2)}) copy-start(f32[128]{0:T(128)} %copy-done.119) | copy-start | bytes 1540
  177.9 16.4 %copy-start.127 = (f32[128]{0:T(128)S(1)}, f32[128]{0:T(128)}, u32[]{:S(2)}) copy-start(f32[128]{0:T(128)} %copy-done.125) | copy-start | bytes 1540
  179.8 15.3 %copy-start.62 = (f32[128,576]{1,0:T(8,128)S(1)}, f32[128,576]{1,0:T(8,128)}, u32[]{:S(2)}) copy-start(f32[128,576]{1,0:T(8,128)} %get-tuple-element.287) | copy-start | bytes 884740
  179.8 15.3 %copy-start.134 = (f32[128]{0:T(128)S(1)}, f32[128]{0:T(128)}, u32[]{:S(2)}) copy-start(f32[128]{0:T(128)} %get-tuple-element.329) | copy-start | bytes 1540
  180.3 23.9 %copy-start.103 = (bf16[128,3,64]{0,2,1:T(8,128)(2,1)}, bf16[128,3,64]{0,2,1:T(8,128)(2,1)S(1)}, u32[]{:S(2)}) copy-start(bf16[128,3,64]{0,2,1:T(8,128)(2,1)S(1)} %maximum_convert_fusion.2) | copy-start | bytes 147460
  195.1 9.1 %copy-start.139 = (f32[128]{0:T(128)}, f32[128]{0:T(128)S(1)}, u32[]{:S(2)}) copy-start(f32[128]{0:T(128)S(1)} %broadcast_multiply_fusion.2) | copy-start | bytes 1540
  196.0 122.9 %collective-permute-start.1 = (bf16[128,576]{1,0:T(8,128)(2,1)}, bf16[128,576]{1,0:T(8,128)(2,1)}, u32[]{:S(2)}, u32[]{:S(2)}) collective-permute-start(bf16[128,576]{1,0:T(8,128)(2,1)} %fusion.89), channel_id=1, source_target_pairs={{16,0},{17,1},{18,2},{19,3},{20,4},{21,5},{22,6},{23,7},{24,8},{25... | collective-permute-start | bytes 442376 | tf_op jit(solution)/shard_map/ppermute | solution.py:423
  225.0 93.9 %copy-start.95 = (f32[128,1536]{1,0:T(8,128)S(1)}, f32[128,1536]{1,0:T(8,128)}, u32[]{:S(2)}) copy-start(f32[128,1536]{1,0:T(8,128)} %copy-done.94) | copy-start | bytes 2359300
  233.9 85.1 %copy-start.41 = (bf16[4,384,576]{2,1,0:T(8,128)(2,1)S(1)}, bf16[4,384,576]{2,1,0:T(8,128)(2,1)}, u32[]{:S(2)}) copy-start(bf16[4,384,576]{2,1,0:T(8,128)(2,1)} %get-tuple-element.214) | copy-start | bytes 5308420
  233.9 85.1 %copy-start.91 = (f32[128,1536]{1,0:T(8,128)S(1)}, f32[128,1536]{1,0:T(8,128)}, u32[]{:S(2)}) copy-start(f32[128,1536]{1,0:T(8,128)} %get-tuple-element.338) | copy-start | bytes 2359300
  233.9 85.1 %copy-start.93 = (f32[128,1536]{1,0:T(8,128)S(1)}, f32[128,1536]{1,0:T(8,128)}, u32[]{:S(2)}) copy-start(f32[128,1536]{1,0:T(8,128)} %copy-done.92) | copy-start | bytes 2359300
  330.1 17.1 %copy-start.109 = (f32[128,32]{0,1:T(8,128)S(1)}, f32[128,32]{0,1:T(8,128)}, u32[]{:S(2)}) copy-start(f32[128,32]{0,1:T(8,128)} %get-tuple-element.326) | copy-start | bytes 49156
  331.2 16.1 %copy-start.86 = (f32[3,64,128,3]{2,1,3,0:T(8,128)S(1)}, f32[3,64,128,3]{2,1,3,0:T(8,128)}, u32[]{:S(2)}) copy-start(f32[3,64,128,3]{2,1,3,0:T(8,128)} %convolution_multiply_fusion) | copy-start | bytes 884740
  332.4 16.2 %copy-start.80 = (bf16[128,576]{1,0:T(8,128)(2,1)S(1)}, bf16[128,576]{1,0:T(8,128)(2,1)}, u32[]{:S(2)}) copy-start(bf16[128,576]{1,0:T(8,128)(2,1)} %copy-done.79) | copy-start | bytes 442372
  (125 other events, 213.8 us)
